TPU v7x, 128 devices: a whole 4x4x4 slice. The times are simulated.
128 devices in a mesh: group: 4 (over x_lo, core), blk: 32 (over z, y, x_hi).
Axes of the slice: x: 4 (x_hi: 2, x_lo: 2; x = x_hi * 2 + x_lo), y: 4, z: 4, core: 2. Of those that a mesh axis runs over, the one named last changes fastest.
Arguments:
- image_emb: bfloat16 [49152, 1280], P(('group', 'blk')), may hold values from -6 to 6
- text_emb: bfloat16 [49152, 1280], P(('group', 'blk')), may hold values from -1 to 1
- positive: int32 [49152], P(('group', 'blk')), may hold values from 0 to 383, as said below
- logit_scale: float32 [1], replicated, may hold values from 10 to 20
Outputs:
- loss: float32 [1], replicated
- image_grad: float32 [49152, 1280], P(('group', 'blk'))
- text_grad: float32 [49152, 1280], P(('group', 'blk'))
Inputs may be any that keep to these rules, and one draw needn't show every extreme that they name: `positive`: within every aligned block of 384 rows the values are a permutation of 0 to 383.
All inputs are finite; a program needn't handle non-finite values.
Results may differ from a plain program's by a relative error of at most 0.0022.
Values may be sent and summed in bfloat16 or wider, within the bound.
A program may use at most 128 MiB of HBM per device.

v0:
```python
import jax
import jax.numpy as jnp
from jax import lax
from jax.sharding import PartitionSpec as P

WIN = 8


def from_behind(block, axis, distance):
    devices = range(lax.axis_size(axis))
    route = [((i - distance) % len(devices), i) for i in devices]
    return lax.ppermute(block, axis, route)


def block_scores(left_rows, right_rows, factor):
    return factor * jnp.dot(left_rows, right_rows.T, preferred_element_type=jnp.float32)


def merge_rows(old_peak, old_total, score_block):
    new_peak = jnp.maximum(old_peak, jnp.max(score_block, axis=1))
    new_total = old_total * jnp.exp(old_peak - new_peak) + jnp.sum(
        jnp.exp(score_block - new_peak[:, None]), axis=1
    )
    return (new_peak, new_total)


def merge_columns(old_peak, old_total, score_block):
    new_peak = jnp.maximum(old_peak, jnp.max(score_block, axis=0))
    new_total = old_total * jnp.exp(old_peak - new_peak) + jnp.sum(
        jnp.exp(score_block - new_peak[None, :]), axis=0
    )
    return (new_peak, new_total)


def on_device(image_emb, text_emb, positive, logit_scale):
    factor = logit_scale[0]
    row_count = image_emb.shape[0]
    batch_size = row_count * lax.axis_size("group") * lax.axis_size("blk")
    columns = jnp.arange(row_count, dtype=jnp.int32)
    pair_mask = (columns[None, :] == positive[:, None]).astype(jnp.float32)
    own_scores = block_scores(image_emb, text_emb, factor)
    chosen = jnp.sum(own_scores * pair_mask)
    row_peak = jnp.max(own_scores, axis=1)
    row_total = jnp.sum(jnp.exp(own_scores - row_peak[:, None]), axis=1)
    col_peak = jnp.max(own_scores, axis=0)
    col_total = jnp.sum(jnp.exp(own_scores - col_peak[None, :]), axis=0)
    text_seen = [text_emb]
    moving_text = text_emb
    moving_peak, moving_total = (col_peak, col_total)
    for rotation in range(1, WIN):
        if rotation == 1:
            moving_text = from_behind(moving_text, "group", 1)
            moving_peak, moving_total = from_behind((moving_peak, moving_total), "group", 1)
        else:
            moving_text = from_behind(moving_text, "blk", 1)
            moving_peak, moving_total = from_behind((moving_peak, moving_total), "blk", 1)
        text_seen.append(moving_text)
        scores = block_scores(image_emb, moving_text, factor)
        row_peak, row_total = merge_rows(row_peak, row_total, scores)
        moving_peak, moving_total = merge_columns(moving_peak, moving_total, scores)
    moving_peak, moving_total = from_behind((moving_peak, moving_total), "blk", 2 - WIN)
    moving_peak, moving_total = from_behind((moving_peak, moving_total), "group", -1)
    col_lse = moving_peak + jnp.log(moving_total)
    row_lse = row_peak + jnp.log(row_total)
    local_terms = jnp.sum(row_lse) + jnp.sum(col_lse) - 2.0 * chosen
    loss_value = lax.psum(local_terms, ("group", "blk")) / (2.0 * batch_size)
    loss = jnp.reshape(loss_value, (1,))
    own_weight = (
        jnp.exp(own_scores - row_lse[:, None])
        + jnp.exp(own_scores - col_lse[None, :])
        - 2.0 * pair_mask
    ).astype(jnp.bfloat16)
    image_total = jnp.dot(own_weight, text_emb, preferred_element_type=jnp.float32)
    own_text_part = jnp.dot(own_weight.T, image_emb, preferred_element_type=jnp.float32)
    moving_lse, moving_sum = (col_lse, own_text_part)
    for rotation in range(1, WIN):
        moving_text = text_seen[rotation]
        if rotation == 1:
            moving_lse, moving_sum = from_behind((moving_lse, moving_sum), "group", 1)
        else:
            moving_lse, moving_sum = from_behind((moving_lse, moving_sum), "blk", 1)
        scores = block_scores(image_emb, moving_text, factor)
        weight = (
            jnp.exp(scores - row_lse[:, None]) + jnp.exp(scores - moving_lse[None, :])
        ).astype(jnp.bfloat16)
        image_total = image_total + jnp.dot(weight, moving_text, preferred_element_type=jnp.float32)
        moving_sum = moving_sum + jnp.dot(weight.T, image_emb, preferred_element_type=jnp.float32)
    moving_sum = from_behind(moving_sum, "blk", 2 - WIN)
    text_total = from_behind(moving_sum, "group", -1)
    return (loss, factor * image_total, factor * text_total)


def solution(mesh):
    placed = (P(("group", "blk"), None), P(("group", "blk"), None), P(("group", "blk")), P())
    return jax.shard_map(
        on_device,
        mesh=mesh,
        in_specs=placed,
        out_specs=(P(), P(("group", "blk"), None), P(("group", "blk"), None)),
        check_vma=False,
    )
```

profile of v0, /device:TPU:24, one launch (start us, length us, event | category | flops | bytes accessed | tf_op | source)
XLA Modules:
  0.0 705.1 jit_solution(13125690471826600917)
XLA Ops:
  0.7 13.7 %collective-permute-done = bf16[384,1280]{1,0:T(8,128)(2,1)S(1)} collective-permute-done((bf16[384,1280]{1,0:T(8,128)(2,1)}, bf16[384,1280]{1,0:T(8,128)(2,1)S(1)}, u32[]{:S(2)}, u32[]{:S(2)}) %collective-permute-start) | collective-permute-done | bytes 983072 | tf_op jit(solution)/shard_map/ppermute | solution.py:12
  14.5 3.0 collective-permute-start.1
  17.5 22.3 %collective-permute-done.1 = bf16[384,1280]{1,0:T(8,128)(2,1)S(1)} collective-permute-done((bf16[384,1280]{1,0:T(8,128)(2,1)S(1)}, bf16[384,1280]{1,0:T(8,128)(2,1)S(1)}, u32[]{:S(2)}, u32[]{:S(2)}) %collective-permute-start.1) | collective-permute-done | bytes 983072 | tf_op jit(solution)/shard_map/ppermute | solution.py:12
  39.8 1.8 collective-permute-start.2
  41.6 22.5 %collective-permute-done.2 = bf16[384,1280]{1,0:T(8,128)(2,1)S(1)} collective-permute-done((bf16[384,1280]{1,0:T(8,128)(2,1)S(1)}, bf16[384,1280]{1,0:T(8,128)(2,1)S(1)}, u32[]{:S(2)}, u32[]{:S(2)}) %collective-permute-start.2) | collective-permute-done | bytes 983072 | tf_op jit(solution)/shard_map/ppermute | solution.py:12
  64.1 1.8 collective-permute-start.3
  65.9 21.7 %collective-permute-done.3 = bf16[384,1280]{1,0:T(8,128)(2,1)S(1)} collective-permute-done((bf16[384,1280]{1,0:T(8,128)(2,1)S(1)}, bf16[384,1280]{1,0:T(8,128)(2,1)S(1)}, u32[]{:S(2)}, u32[]{:S(2)}) %collective-permute-start.3) | collective-permute-done | bytes 983072 | tf_op jit(solution)/shard_map/ppermute | solution.py:12
  87.6 3.9 collective-permute-start.4
  92.1 18.0 %collective-permute-done.4 = bf16[384,1280]{1,0:T(8,128)(2,1)S(1)} collective-permute-done((bf16[384,1280]{1,0:T(8,128)(2,1)S(1)}, bf16[384,1280]{1,0:T(8,128)(2,1)S(1)}, u32[]{:S(2)}, u32[]{:S(2)}) %collective-permute-start.4) | collective-permute-done | bytes 983072 | tf_op jit(solution)/shard_map/ppermute | solution.py:12
  110.1 6.0 collective-permute-start.5
  116.1 2.0 fusion.22
  118.2 0.9 select_reduce_fusion
  119.1 0.8 fusion.21
  119.9 3.7 collective-permute-done.7
  123.6 7.6 %collective-permute-start.8 = (f32[384]{0:T(512)S(1)}, f32[384]{0:T(512)S(1)}, u32[]{:S(2)}, u32[]{:S(2)}) collective-permute-start(f32[384]{0:T(512)S(1)} %max.161), channel_id=1, source_target_pairs={{31,0},{0,1},{1,2},{2,3},{3,4},{4,5},{5,6},{6,7},{7,8},{8,9},{9,10... | collective-permute-start | bytes 4616 | tf_op jit(solution)/shard_map/ppermute | solution.py:12
  131.2 0.8 fusion.20
  132.0 0.9 collective-permute-done.8
  132.9 7.0 collective-permute-start.9
  139.9 7.0 collective-permute-start.6
  149.0 15.3 %collective-permute-done.10 = f32[384]{0:T(512)S(1)} collective-permute-done((f32[384]{0:T(512)S(1)}, f32[384]{0:T(512)S(1)}, u32[]{:S(2)}, u32[]{:S(2)}) %collective-permute-start.10) | collective-permute-done | bytes 1568 | tf_op jit(solution)/shard_map/ppermute | solution.py:12
  164.3 3.1 collective-permute-start.11
  168.1 2.1 collective-permute-done.11
  170.3 2.2 collective-permute-start.12
  173.2 3.0 collective-permute-done.12
  176.3 3.9 collective-permute-start.13
  180.1 0.8 fusion.15
  180.9 1.3 collective-permute-done.13
  182.3 20.5 %collective-permute-start.14 = (f32[384]{0:T(512)S(1)}, f32[384]{0:T(512)S(1)}, u32[]{:S(2)}, u32[]{:S(2)}) collective-permute-start(f32[384]{0:T(512)S(1)} %max.167), channel_id=1, source_target_pairs={{6,0},{7,1},{8,2},{9,3},{10,4},{11,5},{12,6},{13,7},{14,8},{15,9},... | collective-permute-start | bytes 4616 | tf_op jit(solution)/shard_map/ppermute | solution.py:12
  203.4 5.7 collective-permute-done.17
  209.4 5.7 collective-permute-done.18
  215.4 5.7 collective-permute-done.19
  221.4 5.7 collective-permute-done.20
  227.4 5.7 collective-permute-done.21
  234.1 5.0 collective-permute-done.22
  239.1 19.9 %collective-permute-start.23 = (f32[384]{0:T(512)S(1)}, f32[384]{0:T(512)S(1)}, u32[]{:S(2)}, u32[]{:S(2)}) collective-permute-start(f32[384]{0:T(512)S(1)} %multiply_add_fusion), channel_id=1, source_target_pairs={{6,0},{7,1},{8,2},{9,3},{10,4},{11,5},{12,6},{13,7},{14,8},{15,9},... | collective-permute-start | bytes 4616 | tf_op jit(solution)/shard_map/ppermute | solution.py:12
  259.0 1.3 collective-permute-done.23
  262.3 0.9 fusion.13
  263.1 1.0 collective-permute-start.32
  264.2 23.1 %collective-permute-done.25 = f32[384]{0:T(512)S(1)} collective-permute-done((f32[384]{0:T(512)S(1)}, f32[384]{0:T(512)S(1)}, u32[]{:S(2)}, u32[]{:S(2)}) %collective-permute-start.25) | collective-permute-done | bytes 1568 | tf_op jit(solution)/shard_map/ppermute | solution.py:12
  287.3 0.8 convolution_add_fusion
  288.3 45.6 %collective-permute-done.26 = f32[384]{0:T(512)S(1)} collective-permute-done((f32[384]{0:T(512)S(1)}, f32[384]{0:T(512)S(1)}, u32[]{:S(2)}, u32[]{:S(2)}) %collective-permute-start.26) | collective-permute-done | bytes 1568 | tf_op jit(solution)/shard_map/ppermute | solution.py:12
  333.8 0.8 fusion.2
  334.8 44.6 %collective-permute-done.27 = f32[384]{0:T(512)S(1)} collective-permute-done((f32[384]{0:T(512)S(1)}, f32[384]{0:T(512)S(1)}, u32[]{:S(2)}, u32[]{:S(2)}) %collective-permute-start.27) | collective-permute-done | bytes 1568 | tf_op jit(solution)/shard_map/ppermute | solution.py:12
  379.4 0.8 fusion.4
  380.3 2.0 collective-permute-start.28
  382.4 41.8 %collective-permute-done.28 = f32[384]{0:T(512)S(1)} collective-permute-done((f32[384]{0:T(512)S(1)}, f32[384]{0:T(512)S(1)}, u32[]{:S(2)}, u32[]{:S(2)}) %collective-permute-start.28) | collective-permute-done | bytes 1568 | tf_op jit(solution)/shard_map/ppermute | solution.py:12
  424.1 0.8 fusion.6
  425.0 4.7 collective-permute-start.29
  429.7 38.2 %collective-permute-done.29 = f32[384]{0:T(512)S(1)} collective-permute-done((f32[384]{0:T(512)S(1)}, f32[384]{0:T(512)S(1)}, u32[]{:S(2)}, u32[]{:S(2)}) %collective-permute-start.29) | collective-permute-done | bytes 1568 | tf_op jit(solution)/shard_map/ppermute | solution.py:12
  467.9 0.8 fusion.8
  469.2 7.0 collective-permute-start.30
  476.2 34.8 %collective-permute-done.30 = f32[384]{0:T(512)S(1)} collective-permute-done((f32[384]{0:T(512)S(1)}, f32[384]{0:T(512)S(1)}, u32[]{:S(2)}, u32[]{:S(2)}) %collective-permute-start.30) | collective-permute-done | bytes 1568 | tf_op jit(solution)/shard_map/ppermute | solution.py:12
  511.0 0.8 fusion.10
  511.8 3.0 collective-permute-start.38
  514.7 7.0 collective-permute-start.31
  521.7 31.3 %collective-permute-done.31 = f32[384]{0:T(512)S(1)} collective-permute-done((f32[384]{0:T(512)S(1)}, f32[384]{0:T(512)S(1)}, u32[]{:S(2)}, u32[]{:S(2)}) %collective-permute-start.31) | collective-permute-done | bytes 1568 | tf_op jit(solution)/shard_map/ppermute | solution.py:12
  553.0 2.1 fusion.12
  555.1 17.6 %collective-permute-start.39 = (f32[384,1280]{1,0:T(8,128)}, f32[384,1280]{1,0:T(8,128)}, u32[]{:S(2)}, u32[]{:S(2)}) collective-permute-start(f32[384,1280]{1,0:T(8,128)} %fusion.12), channel_id=1, source_target_pairs={{6,0},{7,1},{8,2},{9,3},{10,4},{11,5},{12,6},{13,7},{14,8},{15,9},... | collective-permute-start | bytes 5898248 | tf_op jit(solution)/shard_map/ppermute | solution.py:12
  574.5 99.8 %psum.7 = f32[]{:T(128)} all-reduce(f32[]{:T(128)S(6)} %sub.364), channel_id=1, replica_groups=mesh['group'=4,'blk'=32] {'group','blk'}, use_global_device_ids=true, to_apply=%region_35.0 | all-reduce | flops 1 | bytes 8 | tf_op jit(solution)/shard_map/psum | solution.py:66
  675.0 2.3 fusion.14
  678.1 2.0 collective-permute-start.40
  686.3 2.0 fusion
  688.3 14.3 %collective-permute-done.40 = f32[384,1280]{1,0:T(8,128)S(1)} collective-permute-done((f32[384,1280]{1,0:T(8,128)}, f32[384,1280]{1,0:T(8,128)S(1)}, u32[]{:S(2)}, u32[]{:S(2)}) %collective-permute-start.40) | collective-permute-done | bytes 1966112 | tf_op jit(solution)/shard_map/ppermute | solution.py:12
  702.6 1.4 broadcast_multiply_fusion
  (115 shorter events, 16.5 us)
Async XLA Ops:
  0.6 115.5 %copy-start = (bf16[384,1280]{1,0:T(8,128)(2,1)S(1)}, bf16[384,1280]{1,0:T(8,128)(2,1)}, u32[]{:S(2)}) copy-start(bf16[384,1280]{1,0:T(8,128)(2,1)} %param.4) | copy-start | bytes 2949124
  0.6 117.5 %copy-start.22 = (s32[384]{0:T(512)S(1)}, s32[384]{0:T(512)}, u32[]{:S(2)}) copy-start(s32[384]{0:T(512)} %param.6) | copy-start | bytes 4612
  0.7 13.8 %collective-permute-start = (bf16[384,1280]{1,0:T(8,128)(2,1)}, bf16[384,1280]{1,0:T(8,128)(2,1)S(1)}, u32[]{:S(2)}, u32[]{:S(2)}) collective-permute-start(bf16[384,1280]{1,0:T(8,128)(2,1)} %param.5), channel_id=1, source_target_pairs={{96,0},{0,32},{32,64},{64,96},{97,1},{1,33},{33,65},{65,97},{98,2}... | collective-permute-start | bytes 2949128 | tf_op jit(solution)/shard_map/ppermute | solution.py:12
  14.5 105.4 %copy-start.16 = (bf16[384,1280]{1,0:T(8,128)(2,1)}, bf16[384,1280]{1,0:T(8,128)(2,1)S(1)}, u32[]{:S(2)}) copy-start(bf16[384,1280]{1,0:T(8,128)(2,1)S(1)} %collective-permute-done) | copy-start | bytes 2949124
  14.5 25.3 %collective-permute-start.1 = (bf16[384,1280]{1,0:T(8,128)(2,1)S(1)}, bf16[384,1280]{1,0:T(8,128)(2,1)S(1)}, u32[]{:S(2)}, u32[]{:S(2)}) collective-permute-start(bf16[384,1280]{1,0:T(8,128)(2,1)S(1)} %collective-permute-done), channel_id=1, source_target_pairs={{31,0},{0,1},{1,2},{2,3},{3,4},{4,5},{5,6},{6,7},{7,8},{8,9},{9,10... | collective-permute-start | bytes 2949128 | tf_op jit(solution)/shard_map/ppermute | solution.py:12
  39.8 91.4 %copy-start.10 = (bf16[384,1280]{1,0:T(8,128)(2,1)}, bf16[384,1280]{1,0:T(8,128)(2,1)S(1)}, u32[]{:S(2)}) copy-start(bf16[384,1280]{1,0:T(8,128)(2,1)S(1)} %collective-permute-done.1) | copy-start | bytes 2949124
  39.8 24.4 %collective-permute-start.2 = (bf16[384,1280]{1,0:T(8,128)(2,1)S(1)}, bf16[384,1280]{1,0:T(8,128)(2,1)S(1)}, u32[]{:S(2)}, u32[]{:S(2)}) collective-permute-start(bf16[384,1280]{1,0:T(8,128)(2,1)S(1)} %collective-permute-done.1), channel_id=1, source_target_pairs={{31,0},{0,1},{1,2},{2,3},{3,4},{4,5},{5,6},{6,7},{7,8},{8,9},{9,10... | collective-permute-start | bytes 2949128 | tf_op jit(solution)/shard_map/ppermute | solution.py:12
  64.1 82.8 %copy-start.12 = (bf16[384,1280]{1,0:T(8,128)(2,1)}, bf16[384,1280]{1,0:T(8,128)(2,1)S(1)}, u32[]{:S(2)}) copy-start(bf16[384,1280]{1,0:T(8,128)(2,1)S(1)} %collective-permute-done.2) | copy-start | bytes 2949124
  64.1 23.5 %collective-permute-start.3 = (bf16[384,1280]{1,0:T(8,128)(2,1)S(1)}, bf16[384,1280]{1,0:T(8,128)(2,1)S(1)}, u32[]{:S(2)}, u32[]{:S(2)}) collective-permute-start(bf16[384,1280]{1,0:T(8,128)(2,1)S(1)} %collective-permute-done.2), channel_id=1, source_target_pairs={{31,0},{0,1},{1,2},{2,3},{3,4},{4,5},{5,6},{6,7},{7,8},{8,9},{9,10... | collective-permute-start | bytes 2949128 | tf_op jit(solution)/shard_map/ppermute | solution.py:12
  87.6 60.6 %copy-start.14 = (bf16[384,1280]{1,0:T(8,128)(2,1)}, bf16[384,1280]{1,0:T(8,128)(2,1)S(1)}, u32[]{:S(2)}) copy-start(bf16[384,1280]{1,0:T(8,128)(2,1)S(1)} %collective-permute-done.3) | copy-start | bytes 2949124
  87.6 22.5 %collective-permute-start.4 = (bf16[384,1280]{1,0:T(8,128)(2,1)S(1)}, bf16[384,1280]{1,0:T(8,128)(2,1)S(1)}, u32[]{:S(2)}, u32[]{:S(2)}) collective-permute-start(bf16[384,1280]{1,0:T(8,128)(2,1)S(1)} %collective-permute-done.3), channel_id=1, source_target_pairs={{31,0},{0,1},{1,2},{2,3},{3,4},{4,5},{5,6},{6,7},{7,8},{8,9},{9,10... | collective-permute-start | bytes 2949128 | tf_op jit(solution)/shard_map/ppermute | solution.py:12
  110.1 57.2 %copy-start.18 = (bf16[384,1280]{1,0:T(8,128)(2,1)}, bf16[384,1280]{1,0:T(8,128)(2,1)S(1)}, u32[]{:S(2)}) copy-start(bf16[384,1280]{1,0:T(8,128)(2,1)S(1)} %collective-permute-done.4) | copy-start | bytes 2949124
  110.1 29.8 %collective-permute-start.5 = (bf16[384,1280]{1,0:T(8,128)(2,1)S(1)}, bf16[384,1280]{1,0:T(8,128)(2,1)S(1)}, u32[]{:S(2)}, u32[]{:S(2)}) collective-permute-start(bf16[384,1280]{1,0:T(8,128)(2,1)S(1)} %collective-permute-done.4), channel_id=1, source_target_pairs={{31,0},{0,1},{1,2},{2,3},{3,4},{4,5},{5,6},{6,7},{7,8},{8,9},{9,10... | collective-permute-start | bytes 2949128 | tf_op jit(solution)/shard_map/ppermute | solution.py:12
  118.1 144.2 %copy-start.7 = (f32[384,384]{1,0:T(8,128)}, f32[384,384]{1,0:T(8,128)S(1)}, u32[]{:S(2)}) copy-start(f32[384,384]{1,0:T(8,128)S(1)} %get-tuple-element.53) | copy-start | bytes 1769476
  118.1 5.5 collective-permute-start.7
  119.1 83.9 %collective-permute-start.16 = (f32[384]{0:T(512)S(1)}, f32[384]{0:T(512)S(1)}, u32[]{:S(2)}, u32[]{:S(2)}) collective-permute-start(f32[384]{0:T(512)S(1)} %get-tuple-element.4), channel_id=1, source_target_pairs={{96,0},{0,32},{32,64},{64,96},{97,1},{1,33},{33,65},{65,97},{98,2}... | collective-permute-start | bytes 4616 | tf_op jit(solution)/shard_map/ppermute | solution.py:12
  123.6 9.3 %collective-permute-start.8 = (f32[384]{0:T(512)S(1)}, f32[384]{0:T(512)S(1)}, u32[]{:S(2)}, u32[]{:S(2)}) collective-permute-start(f32[384]{0:T(512)S(1)} %max.161), channel_id=1, source_target_pairs={{31,0},{0,1},{1,2},{2,3},{3,4},{4,5},{5,6},{6,7},{7,8},{8,9},{9,10... | collective-permute-start | bytes 4616 | tf_op jit(solution)/shard_map/ppermute | solution.py:12
  132.9 14.8 %collective-permute-start.9 = (f32[384]{0:T(512)S(1)}, f32[384]{0:T(512)S(1)}, u32[]{:S(2)}, u32[]{:S(2)}) collective-permute-start(f32[384]{0:T(512)S(1)} %max.162), channel_id=1, source_target_pairs={{31,0},{0,1},{1,2},{2,3},{3,4},{4,5},{5,6},{6,7},{7,8},{8,9},{9,10... | collective-permute-start | bytes 4616 | tf_op jit(solution)/shard_map/ppermute | solution.py:12
  139.9 32.5 %copy-start.20 = (bf16[384,1280]{1,0:T(8,128)(2,1)}, bf16[384,1280]{1,0:T(8,128)(2,1)S(1)}, u32[]{:S(2)}) copy-start(bf16[384,1280]{1,0:T(8,128)(2,1)S(1)} %collective-permute-done.5) | copy-start | bytes 2949124
  139.9 40.2 %collective-permute-start.6 = (bf16[384,1280]{1,0:T(8,128)(2,1)S(1)}, bf16[384,1280]{1,0:T(8,128)(2,1)S(1)}, u32[]{:S(2)}, u32[]{:S(2)}) collective-permute-start(bf16[384,1280]{1,0:T(8,128)(2,1)S(1)} %collective-permute-done.5), channel_id=1, source_target_pairs={{31,0},{0,1},{1,2},{2,3},{3,4},{4,5},{5,6},{6,7},{7,8},{8,9},{9,10... | collective-permute-start | bytes 2949128 | tf_op jit(solution)/shard_map/ppermute | solution.py:12
  147.7 16.6 %collective-permute-start.10 = (f32[384]{0:T(512)S(1)}, f32[384]{0:T(512)S(1)}, u32[]{:S(2)}, u32[]{:S(2)}) collective-permute-start(f32[384]{0:T(512)S(1)} %max.163), channel_id=1, source_target_pairs={{31,0},{0,1},{1,2},{2,3},{3,4},{4,5},{5,6},{6,7},{7,8},{8,9},{9,10... | collective-permute-start | bytes 4616 | tf_op jit(solution)/shard_map/ppermute | solution.py:12
  164.3 6.0 collective-permute-start.11
  168.1 299.8 %copy-start.1 = (f32[384,384]{1,0:T(8,128)}, f32[384,384]{1,0:T(8,128)S(1)}, u32[]{:S(2)}) copy-start(f32[384,384]{1,0:T(8,128)S(1)} %get-tuple-element.49) | copy-start | bytes 1769476
  170.3 6.0 collective-permute-start.12
  173.2 337.7 %copy-start.3 = (f32[384,384]{1,0:T(8,128)}, f32[384,384]{1,0:T(8,128)S(1)}, u32[]{:S(2)}) copy-start(f32[384,384]{1,0:T(8,128)S(1)} %get-tuple-element.48) | copy-start | bytes 1769476
  176.3 6.0 collective-permute-start.13
  180.1 23.2 %copy-start.8 = (bf16[384,1280]{1,0:T(8,128)(2,1)}, bf16[384,1280]{1,0:T(8,128)(2,1)S(1)}, u32[]{:S(2)}) copy-start(bf16[384,1280]{1,0:T(8,128)(2,1)S(1)} %collective-permute-done.6) | copy-start | bytes 2949124
  180.9 372.1 %copy-start.5 = (f32[384,384]{1,0:T(8,128)}, f32[384,384]{1,0:T(8,128)S(1)}, u32[]{:S(2)}) copy-start(f32[384,384]{1,0:T(8,128)S(1)} %get-tuple-element.47) | copy-start | bytes 1769476
  182.3 76.8 %collective-permute-start.14 = (f32[384]{0:T(512)S(1)}, f32[384]{0:T(512)S(1)}, u32[]{:S(2)}, u32[]{:S(2)}) collective-permute-start(f32[384]{0:T(512)S(1)} %max.167), channel_id=1, source_target_pairs={{6,0},{7,1},{8,2},{9,3},{10,4},{11,5},{12,6},{13,7},{14,8},{15,9},... | collective-permute-start | bytes 4616 | tf_op jit(solution)/shard_map/ppermute | solution.py:12
  203.0 6.1 collective-permute-start.17
  209.1 6.0 collective-permute-start.18
  215.1 6.0 collective-permute-start.19
  221.1 6.0 collective-permute-start.20
  227.1 6.0 collective-permute-start.21
  233.1 6.0 collective-permute-start.22
  239.1 21.2 %collective-permute-start.23 = (f32[384]{0:T(512)S(1)}, f32[384]{0:T(512)S(1)}, u32[]{:S(2)}, u32[]{:S(2)}) collective-permute-start(f32[384]{0:T(512)S(1)} %multiply_add_fusion), channel_id=1, source_target_pairs={{6,0},{7,1},{8,2},{9,3},{10,4},{11,5},{12,6},{13,7},{14,8},{15,9},... | collective-permute-start | bytes 4616 | tf_op jit(solution)/shard_map/ppermute | solution.py:12
  259.0 2.0 collective-permute-start.15
  260.3 1.3 collective-permute-start.24
  263.1 24.1 %collective-permute-start.32 = (f32[384,1280]{1,0:T(8,128)S(1)}, f32[384,1280]{1,0:T(8,128)S(1)}, u32[]{:S(2)}, u32[]{:S(2)}) collective-permute-start(f32[384,1280]{1,0:T(8,128)S(1)} %fusion.13), channel_id=1, source_target_pairs={{96,0},{0,32},{32,64},{64,96},{97,1},{1,33},{33,65},{65,97},{98,2}... | collective-permute-start | bytes 5898248 | tf_op jit(solution)/shard_map/ppermute | solution.py:12
  264.1 23.2 %collective-permute-start.25 = (f32[384]{0:T(512)S(1)}, f32[384]{0:T(512)S(1)}, u32[]{:S(2)}, u32[]{:S(2)}) collective-permute-start(f32[384]{0:T(512)S(1)} %get-tuple-element.37), channel_id=1, source_target_pairs={{96,0},{0,32},{32,64},{64,96},{97,1},{1,33},{33,65},{65,97},{98,2}... | collective-permute-start | bytes 4616 | tf_op jit(solution)/shard_map/ppermute | solution.py:12
  288.1 45.7 %collective-permute-start.33 = (f32[384,1280]{1,0:T(8,128)S(1)}, f32[384,1280]{1,0:T(8,128)S(1)}, u32[]{:S(2)}, u32[]{:S(2)}) collective-permute-start(f32[384,1280]{1,0:T(8,128)S(1)} %convolution_add_fusion), channel_id=1, source_target_pairs={{31,0},{0,1},{1,2},{2,3},{3,4},{4,5},{5,6},{6,7},{7,8},{8,9},{9,10... | collective-permute-start | bytes 5898248 | tf_op jit(solution)/shard_map/ppermute | solution.py:12
  288.2 45.6 %collective-permute-start.26 = (f32[384]{0:T(512)S(1)}, f32[384]{0:T(512)S(1)}, u32[]{:S(2)}, u32[]{:S(2)}) collective-permute-start(f32[384]{0:T(512)S(1)} %collective-permute-done.25), channel_id=1, source_target_pairs={{31,0},{0,1},{1,2},{2,3},{3,4},{4,5},{5,6},{6,7},{7,8},{8,9},{9,10... | collective-permute-start | bytes 4616 | tf_op jit(solution)/shard_map/ppermute | solution.py:12
  334.6 44.8 %collective-permute-start.34 = (f32[384,1280]{1,0:T(8,128)S(1)}, f32[384,1280]{1,0:T(8,128)S(1)}, u32[]{:S(2)}, u32[]{:S(2)}) collective-permute-start(f32[384,1280]{1,0:T(8,128)S(1)} %fusion.2), channel_id=1, source_target_pairs={{31,0},{0,1},{1,2},{2,3},{3,4},{4,5},{5,6},{6,7},{7,8},{8,9},{9,10... | collective-permute-start | bytes 5898248 | tf_op jit(solution)/shard_map/ppermute | solution.py:12
  334.7 44.7 %collective-permute-start.27 = (f32[384]{0:T(512)S(1)}, f32[384]{0:T(512)S(1)}, u32[]{:S(2)}, u32[]{:S(2)}) collective-permute-start(f32[384]{0:T(512)S(1)} %collective-permute-done.26), channel_id=1, source_target_pairs={{31,0},{0,1},{1,2},{2,3},{3,4},{4,5},{5,6},{6,7},{7,8},{8,9},{9,10... | collective-permute-start | bytes 4616 | tf_op jit(solution)/shard_map/ppermute | solution.py:12
  380.3 43.9 %collective-permute-start.35 = (f32[384,1280]{1,0:T(8,128)S(1)}, f32[384,1280]{1,0:T(8,128)S(1)}, u32[]{:S(2)}, u32[]{:S(2)}) collective-permute-start(f32[384,1280]{1,0:T(8,128)S(1)} %fusion.4), channel_id=1, source_target_pairs={{31,0},{0,1},{1,2},{2,3},{3,4},{4,5},{5,6},{6,7},{7,8},{8,9},{9,10... | collective-permute-start | bytes 5898248 | tf_op jit(solution)/shard_map/ppermute | solution.py:12
  380.3 43.8 %collective-permute-start.28 = (f32[384]{0:T(512)S(1)}, f32[384]{0:T(512)S(1)}, u32[]{:S(2)}, u32[]{:S(2)}) collective-permute-start(f32[384]{0:T(512)S(1)} %collective-permute-done.27), channel_id=1, source_target_pairs={{31,0},{0,1},{1,2},{2,3},{3,4},{4,5},{5,6},{6,7},{7,8},{8,9},{9,10... | collective-permute-start | bytes 4616 | tf_op jit(solution)/shard_map/ppermute | solution.py:12
  425.0 43.0 %collective-permute-start.36 = (f32[384,1280]{1,0:T(8,128)S(1)}, f32[384,1280]{1,0:T(8,128)S(1)}, u32[]{:S(2)}, u32[]{:S(2)}) collective-permute-start(f32[384,1280]{1,0:T(8,128)S(1)} %fusion.6), channel_id=1, source_target_pairs={{31,0},{0,1},{1,2},{2,3},{3,4},{4,5},{5,6},{6,7},{7,8},{8,9},{9,10... | collective-permute-start | bytes 5898248 | tf_op jit(solution)/shard_map/ppermute | solution.py:12
  425.0 42.9 %collective-permute-start.29 = (f32[384]{0:T(512)S(1)}, f32[384]{0:T(512)S(1)}, u32[]{:S(2)}, u32[]{:S(2)}) collective-permute-start(f32[384]{0:T(512)S(1)} %collective-permute-done.28), channel_id=1, source_target_pairs={{31,0},{0,1},{1,2},{2,3},{3,4},{4,5},{5,6},{6,7},{7,8},{8,9},{9,10... | collective-permute-start | bytes 4616 | tf_op jit(solution)/shard_map/ppermute | solution.py:12
  468.7 42.2 %collective-permute-start.37 = (f32[384,1280]{1,0:T(8,128)S(1)}, f32[384,1280]{1,0:T(8,128)S(1)}, u32[]{:S(2)}, u32[]{:S(2)}) collective-permute-start(f32[384,1280]{1,0:T(8,128)S(1)} %fusion.8), channel_id=1, source_target_pairs={{31,0},{0,1},{1,2},{2,3},{3,4},{4,5},{5,6},{6,7},{7,8},{8,9},{9,10... | collective-permute-start | bytes 5898248 | tf_op jit(solution)/shard_map/ppermute | solution.py:12
  469.2 41.8 %collective-permute-start.30 = (f32[384]{0:T(512)S(1)}, f32[384]{0:T(512)S(1)}, u32[]{:S(2)}, u32[]{:S(2)}) collective-permute-start(f32[384]{0:T(512)S(1)} %collective-permute-done.29), channel_id=1, source_target_pairs={{31,0},{0,1},{1,2},{2,3},{3,4},{4,5},{5,6},{6,7},{7,8},{8,9},{9,10... | collective-permute-start | bytes 4616 | tf_op jit(solution)/shard_map/ppermute | solution.py:12
  511.8 41.2 %collective-permute-start.38 = (f32[384,1280]{1,0:T(8,128)S(1)}, f32[384,1280]{1,0:T(8,128)S(1)}, u32[]{:S(2)}, u32[]{:S(2)}) collective-permute-start(f32[384,1280]{1,0:T(8,128)S(1)} %fusion.10), channel_id=1, source_target_pairs={{31,0},{0,1},{1,2},{2,3},{3,4},{4,5},{5,6},{6,7},{7,8},{8,9},{9,10... | collective-permute-start | bytes 5898248 | tf_op jit(solution)/shard_map/ppermute | solution.py:12
  514.7 38.3 %collective-permute-start.31 = (f32[384]{0:T(512)S(1)}, f32[384]{0:T(512)S(1)}, u32[]{:S(2)}, u32[]{:S(2)}) collective-permute-start(f32[384]{0:T(512)S(1)} %collective-permute-done.30), channel_id=1, source_target_pairs={{31,0},{0,1},{1,2},{2,3},{3,4},{4,5},{5,6},{6,7},{7,8},{8,9},{9,10... | collective-permute-start | bytes 4616 | tf_op jit(solution)/shard_map/ppermute | solution.py:12
  555.1 123.0 %collective-permute-start.39 = (f32[384,1280]{1,0:T(8,128)}, f32[384,1280]{1,0:T(8,128)}, u32[]{:S(2)}, u32[]{:S(2)}) collective-permute-start(f32[384,1280]{1,0:T(8,128)} %fusion.12), channel_id=1, source_target_pairs={{6,0},{7,1},{8,2},{9,3},{10,4},{11,5},{12,6},{13,7},{14,8},{15,9},... | collective-permute-start | bytes 5898248 | tf_op jit(solution)/shard_map/ppermute | solution.py:12
  675.0 2.3 copy-start.17
  677.3 2.8 copy-start.11
  678.1 2.8 copy-start.13
  678.1 24.5 %collective-permute-start.40 = (f32[384,1280]{1,0:T(8,128)}, f32[384,1280]{1,0:T(8,128)S(1)}, u32[]{:S(2)}, u32[]{:S(2)}) collective-permute-start(f32[384,1280]{1,0:T(8,128)} %collective-permute-done.39), channel_id=1, source_target_pairs={{32,0},{64,32},{96,64},{0,96},{33,1},{65,33},{97,65},{1,97},{34,2}... | collective-permute-start | bytes 5898248 | tf_op jit(solution)/shard_map/ppermute | solution.py:12
  680.9 1.2 copy-start.15
  682.1 1.1 copy-start.2
  682.1 1.4 copy-start.19
  683.5 1.1 copy-start.4
  683.5 1.4 copy-start.21
  684.9 1.1 copy-start.6
  684.9 1.4 copy-start.9
where the time goes:
time: 709 us; the launch traced here: 705 us
  waiting for transfers between devices  434 us (61%)
  starting transfers between devices  134 us (19%)
  blocking collectives  99.8 us (14%)
  matrix products  24 us (3%)
    ppermute x41, waiting for transfers between devices, from_behind(): return lax.ppermute(block, axis, route)  434 us
    ppermute x41, starting transfers between devices, from_behind(): return lax.ppermute(block, axis, route)  134 us
    psum x1, blocking collectives, on_device(): loss_value = lax.psum(local_terms, ('group', 'blk')) / (2.0 * batch_size)  99.8 us
  transfers between devices with their start and end apart: 41, of which 27 were waited for; matrix products, arithmetic and copies ran while one was open for 3% of the time, Pallas kernels for 0%

commit v1 on v0

v1 whole, which is shorter than its diff:
```python
import functools

import jax
import jax.numpy as jnp
from jax import lax
from jax.experimental import pallas as pl
from jax.experimental.pallas import tpu as pltpu
from jax.sharding import PartitionSpec as P

MESH = pl.DeviceIdType.MESH
F32 = jnp.float32
BF16 = jnp.bfloat16
R = 384
D = 1280
H = D // 2
NC = 4
CH = R // NC
ST = 48
LOW = -1e30
RING = 16


def rcopy(src, dst, ss, rs, dev):
    return pltpu.make_async_remote_copy(
        src_ref=src, dst_ref=dst, send_sem=ss, recv_sem=rs, device_id=dev, device_id_type=MESH
    )


def dot_t(a, b):
    return lax.dot_general(a, b, (((1,), (1,)), ((), ())), preferred_element_type=F32)


def dot_n(a, b):
    return lax.dot_general(a, b, (((1,), (0,)), ((), ())), preferred_element_type=F32)


def merge(parts):
    peak = functools.reduce(jnp.maximum, [m for m, _ in parts])
    total = sum(s * jnp.exp(m - peak) for m, s in parts)
    return peak, total


def tile_of(peak, total):
    row = lax.broadcasted_iota(jnp.int32, (8, peak.shape[1]), 0)
    return jnp.where(row == 0, peak, total)


def pair_of(tile):
    return tile[0:1, :], tile[1:2, :]


def kernel(
    scale_ref, image_ref, text_ref, pos_ref,
    terms_ref, image_out, text_out,
    texts, images, scores, own_scores, weights, weights_t, own_weights_t,
    packed, col_column, row_part, row_diag, col_part, col_diag,
    row_peer, row_owner, row_back, col_peer,
    part1, part2, part3, stash1, stash3, part_in, half_in,
    grad_send, grad_in, image_acc, text_acc,
    local_sem, fetch_ss, fetch_rs, fwd_ss, relay_ss, img_ss, img_rs,
    row_ss, row_rs, col_ss, col_rs,
    half_ss, half_rs, part_ss, part_rs, back_ss, grad_ss, grad_rs,
):
    group = lax.axis_index("group")
    blk = lax.axis_index("blk")
    xh = blk % 2
    big_y = blk // 2
    y = big_y % 4
    factor = scale_ref[0]

    def at_row(step):
        return (group, ((big_y + step + RING) % RING) * 2 + xh)

    up, down = at_row(1), at_row(-1)
    behind = (group + 3) % 4
    ahead = (group + 1) % 4
    same, other = blk, big_y * 2 + (1 - xh)
    handler_same, handler_other = (behind, same), (behind, other)
    owner_same, owner_other = (ahead, same), (ahead, other)
    peer = (group, other)

    text_copy = pltpu.make_async_copy(text_ref, texts.at[0], local_sem.at[0])
    image_copy = pltpu.make_async_copy(image_ref, images.at[pl.ds(2 * R, R)], local_sem.at[1])
    text_copy.start()
    image_copy.start()

    barrier = pltpu.get_barrier_semaphore()
    partners = [at_row(s) for s in (1, 2, 3, 4, -1, -2, -3, -4)]
    partners += [handler_same, handler_other, owner_same, owner_other, peer]
    for dev in partners:
        pl.semaphore_signal(barrier, inc=1, device_id=dev, device_id_type=MESH)
    pl.semaphore_wait(barrier, len(partners))

    def part_of(ref, slot, half, c):
        return ref.at[slot, pl.ds(c * CH, CH), pl.ds(half * H, H)]

    wrap_up = y // 3
    up_slot = 1 + 3 * wrap_up
    up_far = at_row(1 + 3 * wrap_up)
    far = at_row(3)

    def own_copy(stream, slot, half, c, dev):
        return rcopy(
            part_of(texts, 0, half, c), part_of(texts, slot, half, c),
            fetch_ss.at[stream, c], fetch_rs.at[slot, half, c], dev,
        )

    def arrived(slot, half, c):
        ref = part_of(texts, slot, half, c)
        rcopy(ref, ref, fetch_ss.at[0, c], fetch_rs.at[slot, half, c], up).wait_recv()

    def fwd_copy(stream, slot, half, c, dev):
        return rcopy(
            part_of(texts, slot, half, c), part_of(texts, 2, half, c),
            fwd_ss.at[stream, c], fetch_rs.at[2, half, c], dev,
        )

    def relay_copy(half, c):
        return rcopy(
            part_of(texts, 4, half, c), part_of(texts, 1, half, c),
            relay_ss.at[half, c], fetch_rs.at[1, half, c], at_row(-3),
        )

    text_copy.wait()
    for c in range(NC):
        own_copy(0, up_slot, 0, c, up_far).start()
        own_copy(1, 3, 1, c, far).start()
    image_copy.wait()
    own_image = images.at[pl.ds(2 * R, R)]
    to_other = rcopy(own_image, images.at[pl.ds(R, R)], img_ss.at[1], img_rs.at[1], handler_other)
    to_same = rcopy(own_image, images.at[pl.ds(0, R)], img_ss.at[0], img_rs.at[0], handler_same)
    to_other.start()
    to_same.start()
    for c in range(NC):
        own_copy(2, up_slot, 1, c, up_far).start()
        own_copy(3, 3, 0, c, far).start()

    def pack_columns(ref, width, rows):
        x = ref[rows, :]
        peak = jnp.max(x, axis=1, keepdims=True)
        total = jnp.sum(jnp.exp(x - peak), axis=1, keepdims=True)
        lane = lax.broadcasted_iota(jnp.int32, (ST, 128), 1)
        packed[rows, :] = jnp.where(lane == 0, peak, total)
        return jnp.max(x, axis=0, keepdims=True)

    def block_stats(ref, width):
        def first(i, peak):
            rows = pl.ds(pl.multiple_of(i * ST, ST), ST)
            return jnp.maximum(peak, pack_columns(ref, width, rows))

        peak = lax.fori_loop(0, R // ST, first, jnp.full((1, width), LOW, F32))

        def second(i, total):
            rows = pl.ds(pl.multiple_of(i * ST, ST), ST)
            return total + jnp.sum(jnp.exp(ref[rows, :] - peak), axis=0, keepdims=True)

        total = lax.fori_loop(0, R // ST, second, jnp.zeros((1, width), F32))
        col_tile = jnp.transpose(packed[...])[0:8, :]
        return (peak, total), col_tile

    own_scores[...] = factor * dot_t(texts[0], images[pl.ds(2 * R, R), :])
    (diag_peak, diag_total), diag_cols = block_stats(own_scores, R)
    row_diag[...] = tile_of(diag_peak, diag_total)
    col_diag[...] = diag_cols

    def forward(c, _):
        @pl.when(y == 3)
        def _():
            arrived(4, 0, c)
            relay_copy(0, c).start()

        arrived(1, 0, c)
        fwd_copy(0, 1, 0, c, up).start()
        arrived(3, 1, c)
        fwd_copy(1, 3, 1, c, down).start()
        return 0

    lax.fori_loop(0, NC, forward, 0)

    @pl.when(y == 3)
    def _():
        def relay(c, _):
            arrived(4, 1, c)
            relay_copy(1, c).start()
            return 0

        lax.fori_loop(0, NC, relay, 0)

    to_other.wait_recv()
    to_same.wait_recv()

    def block_scores(d, row_state):
        def column(n, _):
            cols = pl.ds(pl.multiple_of(n * 256, 256), 256)
            scores[d, :, cols] = factor * dot_t(texts[d], images[cols, :])
            return 0

        lax.fori_loop(0, 3, column, 0)
        if d in (0, 3):
            @pl.when(xh == (1 if d == 0 else 0))
            def _():
                scores[d, :, pl.ds(R, R)] = jnp.full((R, R), LOW, F32)

        stats, cols = block_stats(scores.at[d], 2 * R)
        if d == 0:
            col_part[0] = tile_of(*merge([pair_of(cols), pair_of(col_diag[...])]))
        else:
            col_part[d] = cols
        return stats if row_state is None else merge([row_state, stats])

    state = block_scores(0, None)
    for c in range(NC):
        arrived(1, 1, c)
    state = block_scores(1, state)
    for c in range(NC):
        arrived(3, 0, c)
    state = block_scores(3, state)
    for half in range(2):
        for c in range(NC):
            arrived(2, half, c)
    state = block_scores(2, state)

    both = tile_of(*state)
    row_part[0] = both[:, 0:R]
    row_part[1] = both[:, R:2 * R]
    sends = []
    steps = (1, 2, 3, -1, -2, -3)
    for k, step in enumerate(steps):
        low, high = max(0, -step), min(4, 4 - step)
        sends.append(rcopy(
            col_part.at[pl.ds(low, high - low)],
            col_peer.at[k, pl.ds(low + step, high - low)],
            col_ss.at[k], col_rs.at[k], at_row(step),
        ))
    sends.append(rcopy(row_part, row_peer, row_ss.at[0], row_rs.at[0], peer))
    sends.append(rcopy(row_part.at[0], row_back.at[0], row_ss.at[1], row_rs.at[1], owner_same))
    sends.append(rcopy(row_part.at[1], row_back.at[1], row_ss.at[2], row_rs.at[2], owner_other))
    sends.append(rcopy(row_diag, row_owner.at[0], row_ss.at[3], row_rs.at[3], handler_same))
    sends.append(rcopy(row_diag, row_owner.at[1], row_ss.at[4], row_rs.at[4], handler_other))
    for copy in sends:
        copy.start()
    for copy in sends:
        copy.wait_recv()

    def lse(parts):
        peak, total = merge(parts)
        return peak + jnp.log(total)

    row_lse = jnp.concatenate(
        [lse([pair_of(row_part[k]), pair_of(row_peer[1 - k]), pair_of(row_owner[k])]) for k in range(2)],
        axis=1,
    )
    own_row_lse = lse([pair_of(row_diag[...]), pair_of(row_back[0]), pair_of(row_back[1])])

    def col_lse(d):
        parts = [pair_of(col_part[d])]
        for k, step in enumerate(steps):
            if 0 <= d - step <= 3:
                parts.append(pair_of(col_peer[k, d]))
        value = lse(parts)
        col_column[d] = jnp.transpose(jnp.broadcast_to(value, (128, R)))
        return value

    def block_weights(d):
        def step(i, _):
            rows = pl.ds(pl.multiple_of(i * ST, ST), ST)
            x = scores[d, rows, :]
            col = jnp.concatenate([col_column[d, rows, :]] * (2 * R // 128), axis=1)
            weights[d, rows, pl.ds(0, 2 * R)] = (jnp.exp(x - row_lse) + jnp.exp(x - col)).astype(BF16)
            return 0

        lax.fori_loop(0, R // ST, step, 0)

    def text_part(d, half):
        return dot_n(weights[d, :, pl.ds(0, 2 * R)], images[pl.ds(0, 2 * R), pl.ds(half * H, H)])

    def flip(d):
        def step(i, _):
            rows = pl.ds(pl.multiple_of(i * 128, 128), 128)
            weights_t[rows, pl.ds(d * R, R)] = jnp.transpose(weights[d, :, rows])
            return 0

        lax.fori_loop(0, 6, step, 0)

    wrap_down = 1 - (y + 3) // 4
    down_slot = 2 * wrap_down
    down_far = at_row(-1 - 3 * wrap_down)
    back_far = at_row(-3)

    def cut(ref, half, c):
        return ref.at[pl.ds(c * CH, CH), pl.ds(half * H, H)]

    def half_copy(half, c, dev):
        return rcopy(
            cut(part2, half, c), half_in.at[half, pl.ds(c * CH, CH)],
            half_ss.at[half, c], half_rs.at[half, c], dev,
        )

    def part_copy(ref, stream, slot, half, c, dev):
        return rcopy(
            cut(ref, half, c), part_of(part_in, slot, half, c),
            part_ss.at[stream, half, c], part_rs.at[slot, half, c], dev,
        )

    def part_arrived(slot, half, c):
        ref = part_of(part_in, slot, half, c)
        rcopy(ref, ref, part_ss.at[0, half, c], part_rs.at[slot, half, c], up).wait_recv()

    def back_copy(half, c):
        return rcopy(
            part_of(part_in, 2, half, c), part_of(part_in, 0, half, c),
            back_ss.at[half, c], part_rs.at[0, half, c], at_row(3),
        )

    col_lse(2)
    block_weights(2)
    part2[:, pl.ds(0, H)] = text_part(2, 0).astype(BF16)
    for c in range(NC):
        half_copy(0, c, down).start()
    part2[:, pl.ds(H, H)] = text_part(2, 1).astype(BF16)
    for c in range(NC):
        half_copy(1, c, up).start()
    col_lse(1)
    block_weights(1)
    part1[:, pl.ds(H, H)] = text_part(1, 1).astype(BF16)
    for c in range(NC):
        part_copy(part1, 0, down_slot, 1, c, down_far).start()
    col_lse(3)
    block_weights(3)
    part3[:, pl.ds(0, H)] = text_part(3, 0).astype(BF16)
    for c in range(NC):
        part_copy(part3, 1, 1, 0, c, back_far).start()
    stash1[...] = text_part(1, 0)
    stash3[...] = text_part(3, 1)
    own_col_lse = col_lse(0)
    block_weights(0)
    for d in range(4):
        flip(d)

    def image_part(k):
        def column(n, _):
            cols = pl.ds(pl.multiple_of(n * 256, 256), 256)
            total = dot_n(weights_t[pl.ds(k * R, R), pl.ds(0, R)], texts[0, :, cols])
            for d in range(1, 4):
                total += dot_n(weights_t[pl.ds(k * R, R), pl.ds(d * R, R)], texts[d, :, cols])
            grad_send[k, :, cols] = total.astype(BF16)
            return 0

        lax.fori_loop(0, 5, column, 0)

    grad_other = rcopy(grad_send.at[1], grad_in.at[1], grad_ss.at[1], grad_rs.at[1], owner_other)
    grad_same = rcopy(grad_send.at[0], grad_in.at[0], grad_ss.at[0], grad_rs.at[0], owner_same)
    image_part(1)
    grad_other.start()
    image_part(0)
    grad_same.start()

    @pl.when(y == 0)
    def _():
        def relay(c, _):
            part_arrived(2, 1, c)
            back_copy(1, c).start()
            return 0

        lax.fori_loop(0, NC, relay, 0)

    def add_halves(c, _):
        rows = pl.ds(pl.multiple_of(c * CH, CH), CH)
        half_copy(0, c, down).wait_recv()
        part1[rows, pl.ds(0, H)] = (stash1[rows, :] + half_in[0, rows, :].astype(F32)).astype(BF16)
        part_copy(part1, 0, down_slot, 0, c, down_far).start()
        half_copy(1, c, up).wait_recv()
        part3[rows, pl.ds(H, H)] = (stash3[rows, :] + half_in[1, rows, :].astype(F32)).astype(BF16)
        part_copy(part3, 1, 1, 1, c, back_far).start()
        return 0

    lax.fori_loop(0, NC, add_halves, 0)

    @pl.when(y == 0)
    def _():
        def relay(c, _):
            part_arrived(2, 0, c)
            back_copy(0, c).start()
            return 0

        lax.fori_loop(0, NC, relay, 0)

    positive = pos_ref[...]
    column = lax.broadcasted_iota(jnp.int32, (R, R), 0)
    mask = column == positive
    x = own_scores[...]
    chosen = jnp.sum(jnp.where(mask, x, 0.0))
    own_col = jnp.concatenate([col_column[0]] * (R // 128), axis=1)
    own_w = jnp.exp(x - own_row_lse) + jnp.exp(x - own_col)
    weights[0, :, pl.ds(2 * R, R)] = jnp.where(mask, own_w - 2.0, own_w).astype(BF16)
    for i in range(3):
        own_weights_t[pl.ds(i * 128, 128), :] = jnp.transpose(weights[0, :, pl.ds(2 * R + i * 128, 128)])
    terms = jnp.sum(own_row_lse) + jnp.sum(own_col_lse) - 2.0 * chosen
    terms_ref[...] = jnp.full((8, 128), terms, F32)

    def own_column(n, _):
        cols = pl.ds(pl.multiple_of(n * 256, 256), 256)
        text_acc[:, cols] = dot_n(weights[0], images[:, cols])
        image_acc[:, cols] = dot_n(own_weights_t[...], texts[0, :, cols])
        return 0

    lax.fori_loop(0, 5, own_column, 0)

    grad_other.wait_recv()
    grad_same.wait_recv()

    def out_copy(acc, out, k, c):
        rows = pl.ds(pl.multiple_of(c * CH, CH), CH)
        return pltpu.make_async_copy(acc.at[rows], out.at[rows], local_sem.at[2 + k * NC + c])

    def finish_image(c, _):
        rows = pl.ds(pl.multiple_of(c * CH, CH), CH)
        image_acc[rows, :] += grad_in[0, rows, :].astype(F32) + grad_in[1, rows, :].astype(F32)
        out_copy(image_acc, image_out, 0, c).start()
        return 0

    lax.fori_loop(0, NC, finish_image, 0)

    def finish_text(c, _):
        rows = pl.ds(pl.multiple_of(c * CH, CH), CH)
        for slot in range(2):
            for half in range(2):
                part_arrived(slot, half, c)
        text_acc[rows, :] += part_in[0, rows, :].astype(F32) + part_in[1, rows, :].astype(F32)
        out_copy(text_acc, text_out, 1, c).start()
        return 0

    lax.fori_loop(0, NC, finish_text, 0)

    to_other.wait_send()
    to_same.wait_send()
    for copy in sends:
        copy.wait_send()
    grad_other.wait_send()
    grad_same.wait_send()

    def drain(c, _):
        own_copy(0, up_slot, 0, c, up_far).wait_send()
        own_copy(1, 3, 1, c, far).wait_send()
        own_copy(2, up_slot, 1, c, up_far).wait_send()
        own_copy(3, 3, 0, c, far).wait_send()
        fwd_copy(0, 1, 0, c, up).wait_send()
        fwd_copy(1, 3, 1, c, down).wait_send()
        half_copy(0, c, down).wait_send()
        half_copy(1, c, up).wait_send()
        for half in range(2):
            part_copy(part1, 0, down_slot, half, c, down_far).wait_send()
            part_copy(part3, 1, 1, half, c, back_far).wait_send()

        @pl.when(y == 3)
        def _():
            relay_copy(0, c).wait_send()
            relay_copy(1, c).wait_send()

        @pl.when(y == 0)
        def _():
            back_copy(0, c).wait_send()
            back_copy(1, c).wait_send()

        out_copy(image_acc, image_out, 0, c).wait()
        out_copy(text_acc, text_out, 1, c).wait()
        return 0

    lax.fori_loop(0, NC, drain, 0)


def on_device(image_emb, text_emb, positive, logit_scale):
    vmem, dma = pltpu.VMEM, pltpu.SemaphoreType.DMA
    terms, image_total, text_total = pl.pallas_call(
        kernel,
        out_shape=(
            jax.ShapeDtypeStruct((8, 128), F32),
            jax.ShapeDtypeStruct((R, D), F32),
            jax.ShapeDtypeStruct((R, D), F32),
        ),
        in_specs=[
            pl.BlockSpec(memory_space=pltpu.SMEM),
            pl.BlockSpec(memory_space=pl.ANY),
            pl.BlockSpec(memory_space=pl.ANY),
            pl.BlockSpec(memory_space=pltpu.VMEM),
        ],
        out_specs=(
            pl.BlockSpec(memory_space=pltpu.VMEM),
            pl.BlockSpec(memory_space=pl.ANY),
            pl.BlockSpec(memory_space=pl.ANY),
        ),
        scratch_shapes=[
            vmem((5, R, D), BF16),
            vmem((3 * R, D), BF16),
            vmem((4, R, 2 * R), F32),
            vmem((R, R), F32),
            vmem((4, R, 3 * R), BF16),
            vmem((2 * R, 4 * R), BF16),
            vmem((R, R), BF16),
            vmem((R, 128), F32),
            vmem((4, R, 128), F32),
            vmem((2, 8, R), F32),
            vmem((8, R), F32),
            vmem((4, 8, R), F32),
            vmem((8, R), F32),
            vmem((2, 8, R), F32),
            vmem((2, 8, R), F32),
            vmem((2, 8, R), F32),
            vmem((6, 4, 8, R), F32),
            vmem((R, D), BF16),
            vmem((R, D), BF16),
            vmem((R, D), BF16),
            vmem((R, H), F32),
            vmem((R, H), F32),
            vmem((3, R, D), BF16),
            vmem((2, R, H), BF16),
            vmem((2, R, D), BF16),
            vmem((2, R, D), BF16),
            vmem((R, D), F32),
            vmem((R, D), F32),
            dma((2 + 2 * NC,)),
            dma((4, NC)),
            dma((5, 2, NC)),
            dma((2, NC)),
            dma((2, NC)),
            dma((2,)),
            dma((2,)),
            dma((5,)),
            dma((5,)),
            dma((6,)),
            dma((6,)),
            dma((2, NC)),
            dma((2, NC)),
            dma((2, 2, NC)),
            dma((3, 2, NC)),
            dma((2, NC)),
            dma((2,)),
            dma((2,)),
        ],
        compiler_params=pltpu.CompilerParams(
            collective_id=0, has_side_effects=True, vmem_limit_bytes=56 * 1024 * 1024
        ),
    )(logit_scale, image_emb, text_emb, positive.reshape(1, R))
    batch_size = R * lax.axis_size("group") * lax.axis_size("blk")
    loss = lax.psum(terms[0, 0:1], ("group", "blk")) / (2.0 * batch_size)
    factor = logit_scale[0]
    return (loss, factor * image_total, factor * text_total)


def solution(mesh):
    placed = (P(("group", "blk"), None), P(("group", "blk"), None), P(("group", "blk")), P())
    return jax.shard_map(
        on_device,
        mesh=mesh,
        in_specs=placed,
        out_specs=(P(), P(("group", "blk"), None), P(("group", "blk"), None)),
        check_vma=False,
    )
```

time: 709 us -> 174 us (0.25)
  waiting for transfers between devices: 434 us -> 0 us
  starting transfers between devices: 134 us -> 0 us
  Pallas kernels: 0 us -> 98.9 us
  blocking collectives: 99.8 us -> 63.6 us
  matrix products: 24 us -> 0 us
    ppermute x41 -> x0, waiting for transfers between devices: 434 us -> none  [from_behind(): return lax.ppermute(block, axis, route)]
    ppermute x41 -> x0, starting transfers between devices: 134 us -> none  [from_behind(): return lax.ppermute(block, axis, route)]
    pallas_call x0 -> x1, Pallas kernels: none -> 98.9 us  [on_device(): pl.pallas_call(kernel, out_shape=(jax.ShapeDtypeStruct((8, 128), F32), ja...]
    psum x1, blocking collectives: 99.8 us -> 63.6 us  [on_device(): loss = lax.psum(terms[0, 0:1], ('group', 'blk')) / (2.0 * batch_size)]
    dot_general x24 -> x0, matrix products: 24 us -> none  [the longest x8 7.4 us: block_scores(): jnp.dot(left_rows, right_rows.T, preferred_element_type=jnp.float32)]
  transfers between devices with their start and end apart: 41 -> 0, of which waited for: 27 -> 0; matrix products, arithmetic and copies ran while one was open for 3% -> 0% of each run, Pallas kernels for 0% -> 0%
where the time goes in v1:
time: 174 us; the launch traced here: 172 us
  Pallas kernels  98.9 us (57%)
  blocking collectives  63.6 us (37%)
  other arithmetic  4.31 us (2%)
  between operations  3.07 us (2%)
  local copies, waits for them, and re-layouts  2.43 us (1%)
    pallas_call x1, Pallas kernels, on_device(): pl.pallas_call(kernel, out_shape=(jax.ShapeDtypeStruct((8, 128), F32), ja...  98.9 us
    psum x1, blocking collectives, on_device(): loss = lax.psum(terms[0, 0:1], ('group', 'blk')) / (2.0 * batch_size)  63.6 us
    mul x1, other arithmetic, on_device(): return (loss, factor * image_total, factor * text_total)  4.31 us

profile of v1, /device:TPU:24, one launch (start us, length us, event | category | flops | bytes accessed | tf_op | source)
XLA Modules:
  0.0 172.3 jit_solution(7874357507483722855)
XLA Ops:
  1.3 1.2 reshape.9.pos_ref
  2.5 98.9 %shard_map.67 = (f32[8,128]{1,0:T(8,128)}, f32[384,1280]{1,0:T(8,128)}, f32[384,1280]{1,0:T(8,128)}) custom-call(f32[1]{0:T(128)} %copy.7.scale_ref, bf16[384,1280]{1,0:T(8,128)(2,1)} %image_ref.1, bf16[384,1280]{1,0:T(8,128)(2,1)} %text_ref.1, s32[1,384]{1,0:T(1,128)} %reshape.9.pos_ref), custom_call_target="tpu_custom_call" | custom-call | tf_op jit(solution)/shard_map/pallas_call | solution.py:474
  101.5 1.2 slice.3
  102.6 63.6 %psum.7 = f32[1]{0:T(128)} all-reduce(f32[1]{0:T(128)} %bitcast), channel_id=1, replica_groups=mesh['group'=4,'blk'=32] {'group','blk'}, use_global_device_ids=true, to_apply=%region_0.0 | all-reduce | flops 1 | bytes 8 | tf_op jit(solution)/shard_map/psum | solution.py:545
  166.8 4.3 %broadcast_multiply_fusion = (f32[384,1280]{1,0:T(8,128)}, f32[384,1280]{1,0:T(8,128)}) fusion(f32[384,1280]{1,0:T(8,128)} %get-tuple-element.8, f32[]{:T(128)} %bitcast.2, f32[384,1280]{1,0:T(8,128)} %get-tuple-element.7), kind=kLoop, calls=%fused_computation | loop fusion | flops 983040 | bytes 7864324 | tf_op jit(solution)/shard_map/mul | solution.py:547

commit v2 on v1

--- a/solution.py
+++ b/solution.py
@@ -51,7 +51,7 @@
 
 def kernel(
     scale_ref, image_ref, text_ref, pos_ref,
-    terms_ref, image_out, text_out,
+    loss_ref, image_out, text_out,
     texts, images, scores, own_scores, weights, weights_t, own_weights_t,
     packed, col_column, row_part, row_diag, col_part, col_diag,
     row_peer, row_owner, row_back, col_peer,
@@ -60,6 +60,7 @@
     local_sem, fetch_ss, fetch_rs, fwd_ss, relay_ss, img_ss, img_rs,
     row_ss, row_rs, col_ss, col_rs,
     half_ss, half_rs, part_ss, part_rs, back_ss, grad_ss, grad_rs,
+    loss_out, loss_in, loss_ss, loss_rs,
 ):
     group = lax.axis_index("group")
     blk = lax.axis_index("blk")
@@ -87,6 +88,8 @@
     barrier = pltpu.get_barrier_semaphore()
     partners = [at_row(s) for s in (1, 2, 3, 4, -1, -2, -3, -4)]
     partners += [handler_same, handler_other, owner_same, owner_other, peer]
+    opposite = ((group + 2) % 4, same)
+    partners += [at_row(8), opposite]
     for dev in partners:
         pl.semaphore_signal(barrier, inc=1, device_id=dev, device_id_type=MESH)
     pl.semaphore_wait(barrier, len(partners))
@@ -159,6 +162,9 @@
         return (peak, total), col_tile
 
     own_scores[...] = factor * dot_t(texts[0], images[pl.ds(2 * R, R), :])
+    positive = pos_ref[...].reshape(1, R)
+    mask = lax.broadcasted_iota(jnp.int32, (R, R), 0) == positive
+    chosen = jnp.sum(jnp.where(mask, own_scores[...], 0.0))
     (diag_peak, diag_total), diag_cols = block_stats(own_scores, R)
     row_diag[...] = tile_of(diag_peak, diag_total)
     col_diag[...] = diag_cols
@@ -242,6 +248,21 @@
     for copy in sends:
         copy.wait_recv()
 
+    mates = [peer, (group + 1 - 2 * (group % 2), same), opposite]
+    for bit in (1, 2, 4, 8):
+        mates.append(at_row(bit - 2 * bit * ((big_y // bit) % 2)))
+
+    def loss_copy(k):
+        return rcopy(loss_out.at[k], loss_in.at[k], loss_ss.at[k], loss_rs.at[k], mates[k])
+
+    def loss_round(k, value=None):
+        if k > 0:
+            loss_copy(k - 1).wait_recv()
+            value = loss_out[k - 1] + loss_in[k - 1]
+        loss_out[k] = value
+        if k < len(mates):
+            loss_copy(k).start()
+
     def lse(parts):
         peak, total = merge(parts)
         return peak + jnp.log(total)
@@ -320,11 +341,15 @@
     part2[:, pl.ds(H, H)] = text_part(2, 1).astype(BF16)
     for c in range(NC):
         half_copy(1, c, up).start()
+    own_col_lse = col_lse(0)
+    terms = jnp.sum(own_row_lse) + jnp.sum(own_col_lse) - 2.0 * chosen
+    loss_round(0, jnp.full((8, 128), terms, F32))
     col_lse(1)
     block_weights(1)
     part1[:, pl.ds(H, H)] = text_part(1, 1).astype(BF16)
     for c in range(NC):
         part_copy(part1, 0, down_slot, 1, c, down_far).start()
+    loss_round(1)
     col_lse(3)
     block_weights(3)
     part3[:, pl.ds(0, H)] = text_part(3, 0).astype(BF16)
@@ -332,7 +357,7 @@
         part_copy(part3, 1, 1, 0, c, back_far).start()
     stash1[...] = text_part(1, 0)
     stash3[...] = text_part(3, 1)
-    own_col_lse = col_lse(0)
+    loss_round(2)
     block_weights(0)
     for d in range(4):
         flip(d)
@@ -352,8 +377,10 @@
     grad_same = rcopy(grad_send.at[0], grad_in.at[0], grad_ss.at[0], grad_rs.at[0], owner_same)
     image_part(1)
     grad_other.start()
+    loss_round(3)
     image_part(0)
     grad_same.start()
+    loss_round(4)
 
     @pl.when(y == 0)
     def _():
@@ -375,6 +402,7 @@
         return 0
 
     lax.fori_loop(0, NC, add_halves, 0)
+    loss_round(5)
 
     @pl.when(y == 0)
     def _():
@@ -385,18 +413,13 @@
 
         lax.fori_loop(0, NC, relay, 0)
 
-    positive = pos_ref[...]
-    column = lax.broadcasted_iota(jnp.int32, (R, R), 0)
-    mask = column == positive
     x = own_scores[...]
-    chosen = jnp.sum(jnp.where(mask, x, 0.0))
     own_col = jnp.concatenate([col_column[0]] * (R // 128), axis=1)
     own_w = jnp.exp(x - own_row_lse) + jnp.exp(x - own_col)
     weights[0, :, pl.ds(2 * R, R)] = jnp.where(mask, own_w - 2.0, own_w).astype(BF16)
     for i in range(3):
         own_weights_t[pl.ds(i * 128, 128), :] = jnp.transpose(weights[0, :, pl.ds(2 * R + i * 128, 128)])
-    terms = jnp.sum(own_row_lse) + jnp.sum(own_col_lse) - 2.0 * chosen
-    terms_ref[...] = jnp.full((8, 128), terms, F32)
+    loss_round(6)
 
     def own_column(n, _):
         cols = pl.ds(pl.multiple_of(n * 256, 256), 256)
@@ -406,6 +429,9 @@
 
     lax.fori_loop(0, 5, own_column, 0)
 
+    loss_round(7)
+    loss_ref[0] = loss_out[7, 0, 0] * (0.5 / (R * 128))
+
     grad_other.wait_recv()
     grad_same.wait_recv()
 
@@ -415,7 +441,9 @@
 
     def finish_image(c, _):
         rows = pl.ds(pl.multiple_of(c * CH, CH), CH)
-        image_acc[rows, :] += grad_in[0, rows, :].astype(F32) + grad_in[1, rows, :].astype(F32)
+        image_acc[rows, :] = factor * (
+            image_acc[rows, :] + grad_in[0, rows, :].astype(F32) + grad_in[1, rows, :].astype(F32)
+        )
         out_copy(image_acc, image_out, 0, c).start()
         return 0
 
@@ -426,7 +454,9 @@
         for slot in range(2):
             for half in range(2):
                 part_arrived(slot, half, c)
-        text_acc[rows, :] += part_in[0, rows, :].astype(F32) + part_in[1, rows, :].astype(F32)
+        text_acc[rows, :] = factor * (
+            text_acc[rows, :] + part_in[0, rows, :].astype(F32) + part_in[1, rows, :].astype(F32)
+        )
         out_copy(text_acc, text_out, 1, c).start()
         return 0
 
@@ -438,6 +468,8 @@
         copy.wait_send()
     grad_other.wait_send()
     grad_same.wait_send()
+    for k in range(len(mates)):
+        loss_copy(k).wait_send()
 
     def drain(c, _):
         own_copy(0, up_slot, 0, c, up_far).wait_send()
@@ -471,10 +503,10 @@
 
 def on_device(image_emb, text_emb, positive, logit_scale):
     vmem, dma = pltpu.VMEM, pltpu.SemaphoreType.DMA
-    terms, image_total, text_total = pl.pallas_call(
+    return pl.pallas_call(
         kernel,
         out_shape=(
-            jax.ShapeDtypeStruct((8, 128), F32),
+            jax.ShapeDtypeStruct((1,), F32),
             jax.ShapeDtypeStruct((R, D), F32),
             jax.ShapeDtypeStruct((R, D), F32),
         ),
@@ -485,7 +517,7 @@
             pl.BlockSpec(memory_space=pltpu.VMEM),
         ],
         out_specs=(
-            pl.BlockSpec(memory_space=pltpu.VMEM),
+            pl.BlockSpec(memory_space=pltpu.SMEM),
             pl.BlockSpec(memory_space=pl.ANY),
             pl.BlockSpec(memory_space=pl.ANY),
         ),
@@ -536,15 +568,15 @@
             dma((2, NC)),
             dma((2,)),
             dma((2,)),
+            vmem((8, 8, 128), F32),
+            vmem((7, 8, 128), F32),
+            dma((7,)),
+            dma((7,)),
         ],
         compiler_params=pltpu.CompilerParams(
-            collective_id=0, has_side_effects=True, vmem_limit_bytes=56 * 1024 * 1024
+            collective_id=0, has_side_effects=True, vmem_limit_bytes=42 * 1024 * 1024
         ),
-    )(logit_scale, image_emb, text_emb, positive.reshape(1, R))
-    batch_size = R * lax.axis_size("group") * lax.axis_size("blk")
-    loss = lax.psum(terms[0, 0:1], ("group", "blk")) / (2.0 * batch_size)
-    factor = logit_scale[0]
-    return (loss, factor * image_total, factor * text_total)
+    )(logit_scale, image_emb, text_emb, positive)
 
 
 def solution(mesh):

time: 174 us -> 113 us (0.65)
  blocking collectives: 63.6 us -> 0 us
  other arithmetic: 4.31 us -> 0 us
  Pallas kernels: 98.9 us -> 103 us
  local copies, waits for them, and re-layouts: 2.43 us -> 5.62 us
    psum x1 -> x0, blocking collectives: 63.6 us -> none  [on_device(): loss = lax.psum(terms[0, 0:1], ('group', 'blk')) / (2.0 * batch_size)]
    unnamed x0 -> x8, local copies, waits for them, and re-layouts: none -> 5.62 us
    pallas_call x1, Pallas kernels: 98.9 us -> 103 us  [on_device(): pl.pallas_call(kernel, out_shape=(jax.ShapeDtypeStruct((1,), F32), jax.Sh...]
    mul x1 -> x0, other arithmetic: 4.31 us -> none  [on_device(): return (loss, factor * image_total, factor * text_total)]
where the time goes in v2:
time: 113 us; the launch traced here: 112 us
  Pallas kernels  103 us (91%)
  local copies, waits for them, and re-layouts  5.62 us (5%)
  between operations  3.03 us (3%)
    pallas_call x1, Pallas kernels, on_device(): pl.pallas_call(kernel, out_shape=(jax.ShapeDtypeStruct((1,), F32), jax.Sh...  103 us
    unnamed x8, local copies, waits for them, and re-layouts  5.62 us

profile of v2, /device:TPU:24, one launch (start us, length us, event | category | flops | bytes accessed | tf_op | source)
XLA Modules:
  0.0 111.9 jit_solution(2361973367324250456)
XLA Ops:
  1.3 0.0 copy-start
  1.3 1.2 %copy-done = bf16[384,1280]{1,0:T(8,128)(2,1)S(1)} copy-done((bf16[384,1280]{1,0:T(8,128)(2,1)S(1)}, bf16[384,1280]{1,0:T(8,128)(2,1)}, u32[]{:S(2)}) %copy-start) | copy-done | bytes 983064
  2.5 0.0 copy-start.1
  2.5 1.2 %copy-done.1 = bf16[384,1280]{1,0:T(8,128)(2,1)S(1)} copy-done((bf16[384,1280]{1,0:T(8,128)(2,1)S(1)}, bf16[384,1280]{1,0:T(8,128)(2,1)}, u32[]{:S(2)}) %copy-start.1) | copy-done | bytes 983064
  3.7 0.0 copy-start.2
  3.7 0.7 copy-done.2
  4.4 103.2 %shard_map.67 = (f32[1]{0:T(128)}, f32[384,1280]{1,0:T(8,128)S(1)}, f32[384,1280]{1,0:T(8,128)S(1)}) custom-call(f32[1]{0:T(128)S(6)} %copy.10.scale_ref, bf16[384,1280]{1,0:T(8,128)(2,1)S(1)} %copy-done, bf16[384,1280]{1,0:T(8,128)(2,1)S(1)} %copy-done.1, s32[384]{0:T(512)S(1)} %copy-done.2), custom_call_target="tpu_custom_call" | custom-call | tf_op jit(solution)/shard_map/pallas_call | solution.py:506
  108.2 1.3 %copy.12 = f32[384,1280]{1,0:T(8,128)} copy(f32[384,1280]{1,0:T(8,128)S(1)} %get-tuple-element.7) | data formatting | bytes 3932160
  109.5 1.3 %copy.13 = f32[384,1280]{1,0:T(8,128)} copy(f32[384,1280]{1,0:T(8,128)S(1)} %get-tuple-element.8) | data formatting | bytes 3932160
Async XLA Ops:
  1.3 1.2 %copy-start = (bf16[384,1280]{1,0:T(8,128)(2,1)S(1)}, bf16[384,1280]{1,0:T(8,128)(2,1)}, u32[]{:S(2)}) copy-start(bf16[384,1280]{1,0:T(8,128)(2,1)} %image_ref.1) | copy-start | bytes 2949124
  2.5 1.2 %copy-start.1 = (bf16[384,1280]{1,0:T(8,128)(2,1)S(1)}, bf16[384,1280]{1,0:T(8,128)(2,1)}, u32[]{:S(2)}) copy-start(bf16[384,1280]{1,0:T(8,128)(2,1)} %text_ref.1) | copy-start | bytes 2949124
  3.7 0.7 copy-start.2

commit v3 on v2

--- a/solution.py
+++ b/solution.py
@@ -13,9 +13,8 @@
 R = 384
 D = 1280
 H = D // 2
-NC = 4
+NC = 3
 CH = R // NC
-ST = 48
 LOW = -1e30
 RING = 16
 
@@ -53,14 +52,14 @@
     scale_ref, image_ref, text_ref, pos_ref,
     loss_ref, image_out, text_out,
     texts, images, scores, own_scores, weights, weights_t, own_weights_t,
-    packed, col_column, row_part, row_diag, col_part, col_diag,
+    col_column, row_part, row_diag, col_part, col_diag,
     row_peer, row_owner, row_back, col_peer,
     part1, part2, part3, stash1, stash3, part_in, half_in,
     grad_send, grad_in, image_acc, text_acc,
     local_sem, fetch_ss, fetch_rs, fwd_ss, relay_ss, img_ss, img_rs,
     row_ss, row_rs, col_ss, col_rs,
     half_ss, half_rs, part_ss, part_rs, back_ss, grad_ss, grad_rs,
-    loss_out, loss_in, loss_ss, loss_rs,
+    loss_out, loss_in, loss_ss, loss_rs, pos_vmem,
 ):
     group = lax.axis_index("group")
     blk = lax.axis_index("blk")
@@ -82,7 +81,9 @@
 
     text_copy = pltpu.make_async_copy(text_ref, texts.at[0], local_sem.at[0])
     image_copy = pltpu.make_async_copy(image_ref, images.at[pl.ds(2 * R, R)], local_sem.at[1])
+    pos_copy = pltpu.make_async_copy(pos_ref, pos_vmem, local_sem.at[2 + 2 * NC])
     text_copy.start()
+    pos_copy.start()
     image_copy.start()
 
     barrier = pltpu.get_barrier_semaphore()
@@ -90,6 +91,8 @@
     partners += [handler_same, handler_other, owner_same, owner_other, peer]
     opposite = ((group + 2) % 4, same)
     partners += [at_row(8), opposite]
+    for step in (4, 8, 12):
+        partners.append((group, ((big_y + step) % RING) * 2 + (1 - xh)))
     for dev in partners:
         pl.semaphore_signal(barrier, inc=1, device_id=dev, device_id_type=MESH)
     pl.semaphore_wait(barrier, len(partners))
@@ -134,40 +137,23 @@
     to_same = rcopy(own_image, images.at[pl.ds(0, R)], img_ss.at[0], img_rs.at[0], handler_same)
     to_other.start()
     to_same.start()
-    for c in range(NC):
-        own_copy(2, up_slot, 1, c, up_far).start()
-        own_copy(3, 3, 0, c, far).start()
-
-    def pack_columns(ref, width, rows):
+
+    def chunk_stats(ref, cols_ref, start, size):
+        rows = pl.ds(start, size)
+        lane = lax.broadcasted_iota(jnp.int32, (size, 128), 1)
         x = ref[rows, :]
         peak = jnp.max(x, axis=1, keepdims=True)
         total = jnp.sum(jnp.exp(x - peak), axis=1, keepdims=True)
-        lane = lax.broadcasted_iota(jnp.int32, (ST, 128), 1)
-        packed[rows, :] = jnp.where(lane == 0, peak, total)
-        return jnp.max(x, axis=0, keepdims=True)
-
-    def block_stats(ref, width):
-        def first(i, peak):
-            rows = pl.ds(pl.multiple_of(i * ST, ST), ST)
-            return jnp.maximum(peak, pack_columns(ref, width, rows))
-
-        peak = lax.fori_loop(0, R // ST, first, jnp.full((1, width), LOW, F32))
-
-        def second(i, total):
-            rows = pl.ds(pl.multiple_of(i * ST, ST), ST)
-            return total + jnp.sum(jnp.exp(ref[rows, :] - peak), axis=0, keepdims=True)
-
-        total = lax.fori_loop(0, R // ST, second, jnp.zeros((1, width), F32))
-        col_tile = jnp.transpose(packed[...])[0:8, :]
-        return (peak, total), col_tile
+        cols_ref[:, rows] = jnp.transpose(jnp.where(lane == 0, peak, total))[0:8, :]
+        row_peak = jnp.max(x, axis=0, keepdims=True)
+        return row_peak, jnp.sum(jnp.exp(x - row_peak), axis=0, keepdims=True)
 
     own_scores[...] = factor * dot_t(texts[0], images[pl.ds(2 * R, R), :])
-    positive = pos_ref[...].reshape(1, R)
+    pos_copy.wait()
+    positive = pos_vmem[...].reshape(1, R)
     mask = lax.broadcasted_iota(jnp.int32, (R, R), 0) == positive
     chosen = jnp.sum(jnp.where(mask, own_scores[...], 0.0))
-    (diag_peak, diag_total), diag_cols = block_stats(own_scores, R)
-    row_diag[...] = tile_of(diag_peak, diag_total)
-    col_diag[...] = diag_cols
+    row_diag[...] = tile_of(*chunk_stats(own_scores, col_diag, 0, R))
 
     def forward(c, _):
         @pl.when(y == 3)
@@ -179,6 +165,8 @@
         fwd_copy(0, 1, 0, c, up).start()
         arrived(3, 1, c)
         fwd_copy(1, 3, 1, c, down).start()
+        own_copy(2, up_slot, 1, c, up_far).start()
+        own_copy(3, 3, 0, c, far).start()
         return 0
 
     lax.fori_loop(0, NC, forward, 0)
@@ -195,36 +183,27 @@
     to_other.wait_recv()
     to_same.wait_recv()
 
-    def block_scores(d, row_state):
-        def column(n, _):
-            cols = pl.ds(pl.multiple_of(n * 256, 256), 256)
-            scores[d, :, cols] = factor * dot_t(texts[d], images[cols, :])
-            return 0
-
-        lax.fori_loop(0, 3, column, 0)
+    def keep_scores(d, start, x):
+        rows = pl.ds(start, x.shape[0])
+        scores[d, rows, :] = factor * x
         if d in (0, 3):
             @pl.when(xh == (1 if d == 0 else 0))
             def _():
-                scores[d, :, pl.ds(R, R)] = jnp.full((R, R), LOW, F32)
-
-        stats, cols = block_stats(scores.at[d], 2 * R)
-        if d == 0:
-            col_part[0] = tile_of(*merge([pair_of(cols), pair_of(col_diag[...])]))
-        else:
-            col_part[d] = cols
-        return stats if row_state is None else merge([row_state, stats])
-
-    state = block_scores(0, None)
+                scores[d, rows, pl.ds(R, R)] = jnp.full((x.shape[0], R), LOW, F32)
+
+        return chunk_stats(scores.at[d], col_part.at[d], start, x.shape[0])
+
+    state = keep_scores(0, 0, dot_t(texts[0], images[pl.ds(0, 2 * R), :]))
+    col_part[0] = tile_of(*merge([pair_of(col_part[0]), pair_of(col_diag[...])]))
     for c in range(NC):
         arrived(1, 1, c)
-    state = block_scores(1, state)
-    for c in range(NC):
         arrived(3, 0, c)
-    state = block_scores(3, state)
-    for half in range(2):
-        for c in range(NC):
-            arrived(2, half, c)
-    state = block_scores(2, state)
+        arrived(2, 0, c)
+        arrived(2, 1, c)
+        rows = pl.ds(c * CH, CH)
+        joined = jnp.concatenate([texts[d, rows, :] for d in (1, 2, 3)], axis=0)
+        x = dot_t(joined, images[pl.ds(0, 2 * R), :])
+        state = merge([state] + [keep_scores(d, c * CH, x[(d - 1) * CH:d * CH, :]) for d in (1, 2, 3)])
 
     both = tile_of(*state)
     row_part[0] = both[:, 0:R]
@@ -248,20 +227,39 @@
     for copy in sends:
         copy.wait_recv()
 
-    mates = [peer, (group + 1 - 2 * (group % 2), same), opposite]
-    for bit in (1, 2, 4, 8):
-        mates.append(at_row(bit - 2 * bit * ((big_y // bit) % 2)))
-
-    def loss_copy(k):
-        return rcopy(loss_out.at[k], loss_in.at[k], loss_ss.at[k], loss_rs.at[k], mates[k])
-
-    def loss_round(k, value=None):
-        if k > 0:
-            loss_copy(k - 1).wait_recv()
-            value = loss_out[k - 1] + loss_in[k - 1]
-        loss_out[k] = value
-        if k < len(mates):
-            loss_copy(k).start()
+    def far_mate(k):
+        place = (big_y // 4 * 2 + xh + k) % 8
+        return (group, (place // 2 * 4 + y) * 2 + place % 2)
+
+    stages = [
+        (group, 4, lambda k: ((group + k) % 4, same)),
+        (y, 4, lambda k: (group, (big_y - y + (y + k) % 4) * 2 + xh)),
+        (big_y // 4 * 2 + xh, 8, far_mate),
+    ]
+
+    def loss_copy(stage, k):
+        place, _, mate = stages[stage]
+        return rcopy(
+            loss_out.at[stage], loss_in.at[stage, place],
+            loss_ss.at[stage, k], loss_rs.at[stage, place], mate(k),
+        )
+
+    def loss_send(stage, value):
+        place, count, _ = stages[stage]
+        loss_out[stage] = value
+        loss_in[stage, place] = value
+        for k in range(1, count):
+            loss_copy(stage, k).start()
+
+    def loss_sum(stage):
+        place, count, _ = stages[stage]
+        for k in range(1, count):
+            other_place = (place + k) % count
+            rcopy(
+                loss_out.at[stage], loss_in.at[stage, other_place],
+                loss_ss.at[stage, k], loss_rs.at[stage, other_place], peer,
+            ).wait_recv()
+        return sum(loss_in[stage, i] for i in range(count))
 
     def lse(parts):
         peak, total = merge(parts)
@@ -283,25 +281,17 @@
         return value
 
     def block_weights(d):
-        def step(i, _):
-            rows = pl.ds(pl.multiple_of(i * ST, ST), ST)
+        for c in range(2):
+            rows = pl.ds(c * (R // 2), R // 2)
             x = scores[d, rows, :]
             col = jnp.concatenate([col_column[d, rows, :]] * (2 * R // 128), axis=1)
             weights[d, rows, pl.ds(0, 2 * R)] = (jnp.exp(x - row_lse) + jnp.exp(x - col)).astype(BF16)
-            return 0
-
-        lax.fori_loop(0, R // ST, step, 0)
 
     def text_part(d, half):
         return dot_n(weights[d, :, pl.ds(0, 2 * R)], images[pl.ds(0, 2 * R), pl.ds(half * H, H)])
 
     def flip(d):
-        def step(i, _):
-            rows = pl.ds(pl.multiple_of(i * 128, 128), 128)
-            weights_t[rows, pl.ds(d * R, R)] = jnp.transpose(weights[d, :, rows])
-            return 0
-
-        lax.fori_loop(0, 6, step, 0)
+        weights_t[:, pl.ds(d * R, R)] = jnp.transpose(weights[d, :, pl.ds(0, 2 * R)])
 
     wrap_down = 1 - (y + 3) // 4
     down_slot = 2 * wrap_down
@@ -343,13 +333,12 @@
         half_copy(1, c, up).start()
     own_col_lse = col_lse(0)
     terms = jnp.sum(own_row_lse) + jnp.sum(own_col_lse) - 2.0 * chosen
-    loss_round(0, jnp.full((8, 128), terms, F32))
+    loss_send(0, jnp.full((8, 128), terms, F32))
     col_lse(1)
     block_weights(1)
     part1[:, pl.ds(H, H)] = text_part(1, 1).astype(BF16)
     for c in range(NC):
         part_copy(part1, 0, down_slot, 1, c, down_far).start()
-    loss_round(1)
     col_lse(3)
     block_weights(3)
     part3[:, pl.ds(0, H)] = text_part(3, 0).astype(BF16)
@@ -357,80 +346,53 @@
         part_copy(part3, 1, 1, 0, c, back_far).start()
     stash1[...] = text_part(1, 0)
     stash3[...] = text_part(3, 1)
-    loss_round(2)
-    block_weights(0)
-    for d in range(4):
-        flip(d)
 
     def image_part(k):
-        def column(n, _):
-            cols = pl.ds(pl.multiple_of(n * 256, 256), 256)
-            total = dot_n(weights_t[pl.ds(k * R, R), pl.ds(0, R)], texts[0, :, cols])
-            for d in range(1, 4):
-                total += dot_n(weights_t[pl.ds(k * R, R), pl.ds(d * R, R)], texts[d, :, cols])
-            grad_send[k, :, cols] = total.astype(BF16)
-            return 0
-
-        lax.fori_loop(0, 5, column, 0)
+        flat = texts.reshape(5 * R, D)[pl.ds(0, 4 * R), :]
+        grad_send[k] = dot_n(weights_t[pl.ds(k * R, R), :], flat).astype(BF16)
 
     grad_other = rcopy(grad_send.at[1], grad_in.at[1], grad_ss.at[1], grad_rs.at[1], owner_other)
     grad_same = rcopy(grad_send.at[0], grad_in.at[0], grad_ss.at[0], grad_rs.at[0], owner_same)
-    image_part(1)
-    grad_other.start()
-    loss_round(3)
-    image_part(0)
-    grad_same.start()
-    loss_round(4)
-
-    @pl.when(y == 0)
-    def _():
-        def relay(c, _):
-            part_arrived(2, 1, c)
-            back_copy(1, c).start()
-            return 0
-
-        lax.fori_loop(0, NC, relay, 0)
-
-    def add_halves(c, _):
-        rows = pl.ds(pl.multiple_of(c * CH, CH), CH)
+    def add_halves(c):
+        rows = pl.ds(c * CH, CH)
         half_copy(0, c, down).wait_recv()
         part1[rows, pl.ds(0, H)] = (stash1[rows, :] + half_in[0, rows, :].astype(F32)).astype(BF16)
         part_copy(part1, 0, down_slot, 0, c, down_far).start()
         half_copy(1, c, up).wait_recv()
         part3[rows, pl.ds(H, H)] = (stash3[rows, :] + half_in[1, rows, :].astype(F32)).astype(BF16)
         part_copy(part3, 1, 1, 1, c, back_far).start()
-        return 0
-
-    lax.fori_loop(0, NC, add_halves, 0)
-    loss_round(5)
-
-    @pl.when(y == 0)
-    def _():
-        def relay(c, _):
-            part_arrived(2, 0, c)
-            back_copy(0, c).start()
-            return 0
-
-        lax.fori_loop(0, NC, relay, 0)
+
+    def relay_parts(half):
+        @pl.when(y == 0)
+        def _():
+            for c in range(NC):
+                part_arrived(2, half, c)
+                back_copy(half, c).start()
+
+    add_halves(0)
+    block_weights(0)
+    for d in range(4):
+        flip(d)
+    image_part(1)
+    grad_other.start()
+    loss_send(1, loss_sum(0))
+    add_halves(1)
+    image_part(0)
+    grad_same.start()
+    add_halves(2)
+    relay_parts(1)
+    loss_send(2, loss_sum(1))
 
     x = own_scores[...]
     own_col = jnp.concatenate([col_column[0]] * (R // 128), axis=1)
     own_w = jnp.exp(x - own_row_lse) + jnp.exp(x - own_col)
     weights[0, :, pl.ds(2 * R, R)] = jnp.where(mask, own_w - 2.0, own_w).astype(BF16)
-    for i in range(3):
-        own_weights_t[pl.ds(i * 128, 128), :] = jnp.transpose(weights[0, :, pl.ds(2 * R + i * 128, 128)])
-    loss_round(6)
-
-    def own_column(n, _):
-        cols = pl.ds(pl.multiple_of(n * 256, 256), 256)
-        text_acc[:, cols] = dot_n(weights[0], images[:, cols])
-        image_acc[:, cols] = dot_n(own_weights_t[...], texts[0, :, cols])
-        return 0
-
-    lax.fori_loop(0, 5, own_column, 0)
-
-    loss_round(7)
-    loss_ref[0] = loss_out[7, 0, 0] * (0.5 / (R * 128))
+    own_weights_t[...] = jnp.transpose(weights[0, :, pl.ds(2 * R, R)])
+    relay_parts(0)
+
+    text_acc[...] = dot_n(weights[0], images[...])
+    image_acc[...] = dot_n(own_weights_t[...], texts[0])
+
 
     grad_other.wait_recv()
     grad_same.wait_recv()
@@ -468,8 +430,10 @@
         copy.wait_send()
     grad_other.wait_send()
     grad_same.wait_send()
-    for k in range(len(mates)):
-        loss_copy(k).wait_send()
+    for stage, (_, count, _) in enumerate(stages):
+        for k in range(1, count):
+            loss_copy(stage, k).wait_send()
+    loss_ref[0] = loss_sum(2)[0, 0] * (0.5 / (R * 128))
 
     def drain(c, _):
         own_copy(0, up_slot, 0, c, up_far).wait_send()
@@ -512,9 +476,9 @@
         ),
         in_specs=[
             pl.BlockSpec(memory_space=pltpu.SMEM),
-            pl.BlockSpec(memory_space=pl.ANY),
-            pl.BlockSpec(memory_space=pl.ANY),
-            pl.BlockSpec(memory_space=pltpu.VMEM),
+            pl.BlockSpec(memory_space=pltpu.HBM),
+            pl.BlockSpec(memory_space=pltpu.HBM),
+            pl.BlockSpec(memory_space=pltpu.HBM),
         ],
         out_specs=(
             pl.BlockSpec(memory_space=pltpu.SMEM),
@@ -529,7 +493,6 @@
             vmem((4, R, 3 * R), BF16),
             vmem((2 * R, 4 * R), BF16),
             vmem((R, R), BF16),
-            vmem((R, 128), F32),
             vmem((4, R, 128), F32),
             vmem((2, 8, R), F32),
             vmem((8, R), F32),
@@ -550,7 +513,7 @@
             vmem((2, R, D), BF16),
             vmem((R, D), F32),
             vmem((R, D), F32),
-            dma((2 + 2 * NC,)),
+            dma((3 + 2 * NC,)),
             dma((4, NC)),
             dma((5, 2, NC)),
             dma((2, NC)),
@@ -568,13 +531,14 @@
             dma((2, NC)),
             dma((2,)),
             dma((2,)),
-            vmem((8, 8, 128), F32),
-            vmem((7, 8, 128), F32),
-            dma((7,)),
-            dma((7,)),
+            vmem((3, 8, 128), F32),
+            vmem((3, 8, 8, 128), F32),
+            dma((3, 8)),
+            dma((3, 8)),
+            vmem((R,), jnp.int32),
         ],
         compiler_params=pltpu.CompilerParams(
-            collective_id=0, has_side_effects=True, vmem_limit_bytes=42 * 1024 * 1024
+            collective_id=0, has_side_effects=True, vmem_limit_bytes=54 * 1024 * 1024
         ),
     )(logit_scale, image_emb, text_emb, positive)
 

time: 113 us -> 104 us (0.920)
  Pallas kernels: 103 us -> 96.6 us
  local copies, waits for them, and re-layouts: 5.62 us -> 4.36 us
    pallas_call x1, Pallas kernels: 103 us -> 96.6 us  [on_device(): pl.pallas_call(kernel, out_shape=(jax.ShapeDtypeStruct((1,), F32), jax.Sh...]
    unnamed x8 -> x4, local copies, waits for them, and re-layouts: 5.62 us -> 4.36 us
where the time goes in v3:
time: 104 us
  Pallas kernels  96.6 us (93%)
  local copies, waits for them, and re-layouts  4.36 us (4%)
  between operations  3.05 us (3%)
    pallas_call x1, Pallas kernels, on_device(): pl.pallas_call(kernel, out_shape=(jax.ShapeDtypeStruct((1,), F32), jax.Sh...  96.6 us
    unnamed x4, local copies, waits for them, and re-layouts  4.36 us

profile of v3, /device:TPU:24, one launch (start us, length us, event | category | flops | bytes accessed | tf_op | source)
XLA Modules:
  0.0 104.0 jit_solution(16178370663452295174)
XLA Ops:
  1.3 96.6 %shard_map.67 = (f32[1]{0:T(128)}, f32[384,1280]{1,0:T(8,128)}, f32[384,1280]{1,0:T(8,128)}) custom-call(f32[1]{0:T(128)S(6)} %copy.10.scale_ref, bf16[384,1280]{1,0:T(8,128)(2,1)} %image_ref.1, bf16[384,1280]{1,0:T(8,128)(2,1)} %text_ref.1, s32[384]{0:T(512)} %pos_ref.1), custom_call_target="tpu_custom_call" | custom-call | tf_op jit(solution)/shard_map/pallas_call | solution.py:470
  98.5 0.0 copy-start
  98.5 3.1 %copy.12 = f32[384,1280]{1,0:T(8,128)} copy(f32[384,1280]{1,0:T(8,128)} %get-tuple-element.7) | data formatting | bytes 3932160
  101.6 0.0 copy-done
  101.6 1.3 %copy.13 = f32[384,1280]{1,0:T(8,128)} copy(f32[384,1280]{1,0:T(8,128)S(1)} %copy-done) | data formatting | bytes 3932160
Async XLA Ops:
  98.5 3.1 %copy-start = (f32[384,1280]{1,0:T(8,128)S(1)}, f32[384,1280]{1,0:T(8,128)}, u32[]{:S(2)}) copy-start(f32[384,1280]{1,0:T(8,128)} %get-tuple-element.8) | copy-start | bytes 5898244

commit v4 on v3

--- a/solution.py
+++ b/solution.py
@@ -87,12 +87,9 @@
     image_copy.start()
 
     barrier = pltpu.get_barrier_semaphore()
-    partners = [at_row(s) for s in (1, 2, 3, 4, -1, -2, -3, -4)]
-    partners += [handler_same, handler_other, owner_same, owner_other, peer]
-    opposite = ((group + 2) % 4, same)
-    partners += [at_row(8), opposite]
-    for step in (4, 8, 12):
-        partners.append((group, ((big_y + step) % RING) * 2 + (1 - xh)))
+    partners = [at_row(step) for step in range(1, RING)]
+    partners += [((group + k) % 4, blk) for k in (1, 2, 3)]
+    partners += [((group + k) % 4, other) for k in range(4)]
     for dev in partners:
         pl.semaphore_signal(barrier, inc=1, device_id=dev, device_id_type=MESH)
     pl.semaphore_wait(barrier, len(partners))
@@ -227,15 +224,11 @@
     for copy in sends:
         copy.wait_recv()
 
-    def far_mate(k):
-        place = (big_y // 4 * 2 + xh + k) % 8
-        return (group, (place // 2 * 4 + y) * 2 + place % 2)
-
-    stages = [
-        (group, 4, lambda k: ((group + k) % 4, same)),
-        (y, 4, lambda k: (group, (big_y - y + (y + k) % 4) * 2 + xh)),
-        (big_y // 4 * 2 + xh, 8, far_mate),
-    ]
+    def near_mate(k):
+        place = (group * 2 + xh + k) % 8
+        return (place // 2, big_y * 2 + place % 2)
+
+    stages = [(group * 2 + xh, 8, near_mate), (big_y, RING, at_row)]
 
     def loss_copy(stage, k):
         place, _, mate = stages[stage]
@@ -339,6 +332,7 @@
     part1[:, pl.ds(H, H)] = text_part(1, 1).astype(BF16)
     for c in range(NC):
         part_copy(part1, 0, down_slot, 1, c, down_far).start()
+    loss_send(1, loss_sum(0))
     col_lse(3)
     block_weights(3)
     part3[:, pl.ds(0, H)] = text_part(3, 0).astype(BF16)
@@ -375,13 +369,11 @@
         flip(d)
     image_part(1)
     grad_other.start()
-    loss_send(1, loss_sum(0))
     add_halves(1)
     image_part(0)
     grad_same.start()
     add_halves(2)
     relay_parts(1)
-    loss_send(2, loss_sum(1))
 
     x = own_scores[...]
     own_col = jnp.concatenate([col_column[0]] * (R // 128), axis=1)
@@ -433,7 +425,7 @@
     for stage, (_, count, _) in enumerate(stages):
         for k in range(1, count):
             loss_copy(stage, k).wait_send()
-    loss_ref[0] = loss_sum(2)[0, 0] * (0.5 / (R * 128))
+    loss_ref[0] = loss_sum(1)[0, 0] * (0.5 / (R * 128))
 
     def drain(c, _):
         own_copy(0, up_slot, 0, c, up_far).wait_send()
@@ -531,10 +523,10 @@
             dma((2, NC)),
             dma((2,)),
             dma((2,)),
-            vmem((3, 8, 128), F32),
-            vmem((3, 8, 8, 128), F32),
-            dma((3, 8)),
-            dma((3, 8)),
+            vmem((2, 8, 128), F32),
+            vmem((2, RING, 8, 128), F32),
+            dma((2, RING)),
+            dma((2, RING)),
             vmem((R,), jnp.int32),
         ],
         compiler_params=pltpu.CompilerParams(

time: 104 us -> 102 us (0.981); the launches traced: 104 us -> 100 us
  Pallas kernels: 96.6 us -> 93 us
    pallas_call x1, Pallas kernels: 96.6 us -> 93 us  [on_device(): pl.pallas_call(kernel, out_shape=(jax.ShapeDtypeStruct((1,), F32), jax.Sh...]
where the time goes in v4:
time: 102 us; the launch traced here: 100 us
  Pallas kernels  93 us (91%)
  local copies, waits for them, and re-layouts  4.36 us (4%)
  between operations  3.05 us (3%)
    pallas_call x1, Pallas kernels, on_device(): pl.pallas_call(kernel, out_shape=(jax.ShapeDtypeStruct((1,), F32), jax.Sh...  93 us
    unnamed x4, local copies, waits for them, and re-layouts  4.36 us

profile of v4, /device:TPU:24, one launch (start us, length us, event | category | flops | bytes accessed | tf_op | source)
XLA Modules:
  0.0 100.4 jit_solution(17481756412016874051)
XLA Ops:
  1.3 93.0 %shard_map.67 = (f32[1]{0:T(128)}, f32[384,1280]{1,0:T(8,128)}, f32[384,1280]{1,0:T(8,128)}) custom-call(f32[1]{0:T(128)S(6)} %copy.10.scale_ref, bf16[384,1280]{1,0:T(8,128)(2,1)} %image_ref.1, bf16[384,1280]{1,0:T(8,128)(2,1)} %text_ref.1, s32[384]{0:T(512)} %pos_ref.1), custom_call_target="tpu_custom_call" | custom-call | tf_op jit(solution)/shard_map/pallas_call | solution.py:462
  94.9 0.0 copy-start
  94.9 3.1 %copy.12 = f32[384,1280]{1,0:T(8,128)} copy(f32[384,1280]{1,0:T(8,128)} %get-tuple-element.7) | data formatting | bytes 3932160
  98.0 0.0 copy-done
  98.0 1.3 %copy.13 = f32[384,1280]{1,0:T(8,128)} copy(f32[384,1280]{1,0:T(8,128)S(1)} %copy-done) | data formatting | bytes 3932160
Async XLA Ops:
  94.9 3.1 %copy-start = (f32[384,1280]{1,0:T(8,128)S(1)}, f32[384,1280]{1,0:T(8,128)}, u32[]{:S(2)}) copy-start(f32[384,1280]{1,0:T(8,128)} %get-tuple-element.8) | copy-start | bytes 5898244

commit v5 on v4

--- a/solution.py
+++ b/solution.py
@@ -55,7 +55,7 @@
     col_column, row_part, row_diag, col_part, col_diag,
     row_peer, row_owner, row_back, col_peer,
     part1, part2, part3, stash1, stash3, part_in, half_in,
-    grad_send, grad_in, image_acc, text_acc,
+    grad_send, grad_in,
     local_sem, fetch_ss, fetch_rs, fwd_ss, relay_ss, img_ss, img_rs,
     row_ss, row_rs, col_ss, col_rs,
     half_ss, half_rs, part_ss, part_rs, back_ss, grad_ss, grad_rs,
@@ -81,7 +81,7 @@
 
     text_copy = pltpu.make_async_copy(text_ref, texts.at[0], local_sem.at[0])
     image_copy = pltpu.make_async_copy(image_ref, images.at[pl.ds(2 * R, R)], local_sem.at[1])
-    pos_copy = pltpu.make_async_copy(pos_ref, pos_vmem, local_sem.at[2 + 2 * NC])
+    pos_copy = pltpu.make_async_copy(pos_ref, pos_vmem, local_sem.at[2])
     text_copy.start()
     pos_copy.start()
     image_copy.start()
@@ -151,6 +151,11 @@
     mask = lax.broadcasted_iota(jnp.int32, (R, R), 0) == positive
     chosen = jnp.sum(jnp.where(mask, own_scores[...], 0.0))
     row_diag[...] = tile_of(*chunk_stats(own_scores, col_diag, 0, R))
+
+    diag_same = rcopy(row_diag, row_owner.at[0], row_ss.at[3], row_rs.at[3], handler_same)
+    diag_other = rcopy(row_diag, row_owner.at[1], row_ss.at[4], row_rs.at[4], handler_other)
+    diag_same.start()
+    diag_other.start()
 
     def forward(c, _):
         @pl.when(y == 3)
@@ -206,7 +211,7 @@
     row_part[0] = both[:, 0:R]
     row_part[1] = both[:, R:2 * R]
     sends = []
-    steps = (1, 2, 3, -1, -2, -3)
+    steps = (-1, 1, 2, -2, 3, -3)
     for k, step in enumerate(steps):
         low, high = max(0, -step), min(4, 4 - step)
         sends.append(rcopy(
@@ -217,11 +222,12 @@
     sends.append(rcopy(row_part, row_peer, row_ss.at[0], row_rs.at[0], peer))
     sends.append(rcopy(row_part.at[0], row_back.at[0], row_ss.at[1], row_rs.at[1], owner_same))
     sends.append(rcopy(row_part.at[1], row_back.at[1], row_ss.at[2], row_rs.at[2], owner_other))
-    sends.append(rcopy(row_diag, row_owner.at[0], row_ss.at[3], row_rs.at[3], handler_same))
-    sends.append(rcopy(row_diag, row_owner.at[1], row_ss.at[4], row_rs.at[4], handler_other))
-    for copy in sends:
+    from_peer, *from_handlers = sends[6:]
+    for copy in [from_peer] + sends[:6] + from_handlers:
         copy.start()
-    for copy in sends:
+    diag_same.wait_recv()
+    diag_other.wait_recv()
+    for copy in [from_peer] + sends[:3]:
         copy.wait_recv()
 
     def near_mate(k):
@@ -262,7 +268,6 @@
         [lse([pair_of(row_part[k]), pair_of(row_peer[1 - k]), pair_of(row_owner[k])]) for k in range(2)],
         axis=1,
     )
-    own_row_lse = lse([pair_of(row_diag[...]), pair_of(row_back[0]), pair_of(row_back[1])])
 
     def col_lse(d):
         parts = [pair_of(col_part[d])]
@@ -324,6 +329,9 @@
     part2[:, pl.ds(H, H)] = text_part(2, 1).astype(BF16)
     for c in range(NC):
         half_copy(1, c, up).start()
+    for copy in sends[3:6] + from_handlers:
+        copy.wait_recv()
+    own_row_lse = lse([pair_of(row_diag[...]), pair_of(row_back[0]), pair_of(row_back[1])])
     own_col_lse = col_lse(0)
     terms = jnp.sum(own_row_lse) + jnp.sum(own_col_lse) - 2.0 * chosen
     loss_send(0, jnp.full((8, 128), terms, F32))
@@ -382,23 +390,18 @@
     own_weights_t[...] = jnp.transpose(weights[0, :, pl.ds(2 * R, R)])
     relay_parts(0)
 
-    text_acc[...] = dot_n(weights[0], images[...])
-    image_acc[...] = dot_n(own_weights_t[...], texts[0])
+    text_out[...] = dot_n(weights[0], images[...])
+    image_out[...] = dot_n(own_weights_t[...], texts[0])
 
 
     grad_other.wait_recv()
     grad_same.wait_recv()
 
-    def out_copy(acc, out, k, c):
-        rows = pl.ds(pl.multiple_of(c * CH, CH), CH)
-        return pltpu.make_async_copy(acc.at[rows], out.at[rows], local_sem.at[2 + k * NC + c])
-
     def finish_image(c, _):
         rows = pl.ds(pl.multiple_of(c * CH, CH), CH)
-        image_acc[rows, :] = factor * (
-            image_acc[rows, :] + grad_in[0, rows, :].astype(F32) + grad_in[1, rows, :].astype(F32)
-        )
-        out_copy(image_acc, image_out, 0, c).start()
+        image_out[rows, :] = factor * (
+            image_out[rows, :] + grad_in[0, rows, :].astype(F32) + grad_in[1, rows, :].astype(F32)
+        )
         return 0
 
     lax.fori_loop(0, NC, finish_image, 0)
@@ -408,17 +411,16 @@
         for slot in range(2):
             for half in range(2):
                 part_arrived(slot, half, c)
-        text_acc[rows, :] = factor * (
-            text_acc[rows, :] + part_in[0, rows, :].astype(F32) + part_in[1, rows, :].astype(F32)
-        )
-        out_copy(text_acc, text_out, 1, c).start()
+        text_out[rows, :] = factor * (
+            text_out[rows, :] + part_in[0, rows, :].astype(F32) + part_in[1, rows, :].astype(F32)
+        )
         return 0
 
     lax.fori_loop(0, NC, finish_text, 0)
 
     to_other.wait_send()
     to_same.wait_send()
-    for copy in sends:
+    for copy in sends + [diag_same, diag_other]:
         copy.wait_send()
     grad_other.wait_send()
     grad_same.wait_send()
@@ -450,8 +452,6 @@
             back_copy(0, c).wait_send()
             back_copy(1, c).wait_send()
 
-        out_copy(image_acc, image_out, 0, c).wait()
-        out_copy(text_acc, text_out, 1, c).wait()
         return 0
 
     lax.fori_loop(0, NC, drain, 0)
@@ -474,8 +474,8 @@
         ],
         out_specs=(
             pl.BlockSpec(memory_space=pltpu.SMEM),
-            pl.BlockSpec(memory_space=pl.ANY),
-            pl.BlockSpec(memory_space=pl.ANY),
+            pl.BlockSpec(memory_space=pltpu.VMEM),
+            pl.BlockSpec(memory_space=pltpu.VMEM),
         ),
         scratch_shapes=[
             vmem((5, R, D), BF16),
@@ -503,9 +503,7 @@
             vmem((2, R, H), BF16),
             vmem((2, R, D), BF16),
             vmem((2, R, D), BF16),
-            vmem((R, D), F32),
-            vmem((R, D), F32),
-            dma((3 + 2 * NC,)),
+            dma((3,)),
             dma((4, NC)),
             dma((5, 2, NC)),
             dma((2, NC)),
@@ -530,9 +528,9 @@
             vmem((R,), jnp.int32),
         ],
         compiler_params=pltpu.CompilerParams(
-            collective_id=0, has_side_effects=True, vmem_limit_bytes=54 * 1024 * 1024
+            collective_id=0, has_side_effects=True, vmem_limit_bytes=42 * 1024 * 1024
         ),
-    )(logit_scale, image_emb, text_emb, positive)
+    )(logit_scale, *(pltpu.with_memory_space_constraint(a, pltpu.HBM) for a in (image_emb, text_emb, positive)))
 
 
 def solution(mesh):

time: 102 us -> 99.1 us (0.972)
  the two profiles are of different devices: /device:TPU:24 before, /device:TPU:1 now
where the time goes in v5:
time: 99.1 us; the launch traced here: 99 us
  Pallas kernels  93.5 us (94%)
  between operations  2.97 us (3%)
  local copies, waits for them, and re-layouts  2.55 us (3%)
    pallas_call x1, Pallas kernels, on_device(): pl.pallas_call(kernel, out_shape=(jax.ShapeDtypeStruct((1,), F32), jax.Sh...  93.5 us
    unnamed x2, local copies, waits for them, and re-layouts  2.55 us

profile of v5, /device:TPU:1, one launch (start us, length us, event | category | flops | bytes accessed | tf_op | source)
XLA Modules:
  0.0 99.0 jit_solution(18349711595446975568)
XLA Ops:
  1.3 93.5 %shard_map.67 = (f32[1]{0:T(128)}, f32[384,1280]{1,0:T(8,128)S(1)}, f32[384,1280]{1,0:T(8,128)S(1)}) custom-call(f32[1]{0:T(128)S(6)} %copy.10.scale_ref, bf16[384,1280]{1,0:T(8,128)(2,1)} %image_ref.1, bf16[384,1280]{1,0:T(8,128)(2,1)} %text_ref.1, s32[384]{0:T(512)} %pos_ref.1), custom_call_target="tpu_custom_call" | custom-call | tf_op jit(solution)/shard_map/pallas_call | solution.py:462
  95.3 1.3 %copy.12 = f32[384,1280]{1,0:T(8,128)} copy(f32[384,1280]{1,0:T(8,128)S(1)} %get-tuple-element.7) | data formatting | bytes 3932160
  96.6 1.3 %copy.13 = f32[384,1280]{1,0:T(8,128)} copy(f32[384,1280]{1,0:T(8,128)S(1)} %get-tuple-element.8) | data formatting | bytes 3932160

commit v6 on v5

--- a/solution.py
+++ b/solution.py
@@ -13,8 +13,10 @@
 R = 384
 D = 1280
 H = D // 2
-NC = 3
+NC = 6
 CH = R // NC
+SC = 128
+PER = NC // 3
 LOW = -1e30
 RING = 16
 
@@ -197,15 +199,16 @@
 
     state = keep_scores(0, 0, dot_t(texts[0], images[pl.ds(0, 2 * R), :]))
     col_part[0] = tile_of(*merge([pair_of(col_part[0]), pair_of(col_diag[...])]))
-    for c in range(NC):
-        arrived(1, 1, c)
-        arrived(3, 0, c)
-        arrived(2, 0, c)
-        arrived(2, 1, c)
-        rows = pl.ds(c * CH, CH)
+    for g in range(R // SC):
+        for c in range(g * PER, (g + 1) * PER):
+            arrived(1, 1, c)
+            arrived(3, 0, c)
+            arrived(2, 0, c)
+            arrived(2, 1, c)
+        rows = pl.ds(g * SC, SC)
         joined = jnp.concatenate([texts[d, rows, :] for d in (1, 2, 3)], axis=0)
         x = dot_t(joined, images[pl.ds(0, 2 * R), :])
-        state = merge([state] + [keep_scores(d, c * CH, x[(d - 1) * CH:d * CH, :]) for d in (1, 2, 3)])
+        state = merge([state] + [keep_scores(d, g * SC, x[(d - 1) * SC:d * SC, :]) for d in (1, 2, 3)])
 
     both = tile_of(*state)
     row_part[0] = both[:, 0:R]
@@ -285,8 +288,8 @@
             col = jnp.concatenate([col_column[d, rows, :]] * (2 * R // 128), axis=1)
             weights[d, rows, pl.ds(0, 2 * R)] = (jnp.exp(x - row_lse) + jnp.exp(x - col)).astype(BF16)
 
-    def text_part(d, half):
-        return dot_n(weights[d, :, pl.ds(0, 2 * R)], images[pl.ds(0, 2 * R), pl.ds(half * H, H)])
+    def text_part(d):
+        return dot_n(weights[d, :, pl.ds(0, 2 * R)], images[pl.ds(0, 2 * R), :])
 
     def flip(d):
         weights_t[:, pl.ds(d * R, R)] = jnp.transpose(weights[d, :, pl.ds(0, 2 * R)])
@@ -323,11 +326,9 @@
 
     col_lse(2)
     block_weights(2)
-    part2[:, pl.ds(0, H)] = text_part(2, 0).astype(BF16)
+    part2[...] = text_part(2).astype(BF16)
     for c in range(NC):
         half_copy(0, c, down).start()
-    part2[:, pl.ds(H, H)] = text_part(2, 1).astype(BF16)
-    for c in range(NC):
         half_copy(1, c, up).start()
     for copy in sends[3:6] + from_handlers:
         copy.wait_recv()
@@ -337,17 +338,19 @@
     loss_send(0, jnp.full((8, 128), terms, F32))
     col_lse(1)
     block_weights(1)
-    part1[:, pl.ds(H, H)] = text_part(1, 1).astype(BF16)
+    whole = text_part(1)
+    part1[:, pl.ds(H, H)] = whole[:, H:].astype(BF16)
+    stash1[...] = whole[:, :H]
     for c in range(NC):
         part_copy(part1, 0, down_slot, 1, c, down_far).start()
     loss_send(1, loss_sum(0))
     col_lse(3)
     block_weights(3)
-    part3[:, pl.ds(0, H)] = text_part(3, 0).astype(BF16)
+    whole = text_part(3)
+    part3[:, pl.ds(0, H)] = whole[:, :H].astype(BF16)
+    stash3[...] = whole[:, H:]
     for c in range(NC):
         part_copy(part3, 1, 1, 0, c, back_far).start()
-    stash1[...] = text_part(1, 0)
-    stash3[...] = text_part(3, 1)
 
     def image_part(k):
         flat = texts.reshape(5 * R, D)[pl.ds(0, 4 * R), :]
@@ -364,31 +367,34 @@
         part3[rows, pl.ds(H, H)] = (stash3[rows, :] + half_in[1, rows, :].astype(F32)).astype(BF16)
         part_copy(part3, 1, 1, 1, c, back_far).start()
 
-    def relay_parts(half):
+    def relay_parts():
         @pl.when(y == 0)
         def _():
             for c in range(NC):
-                part_arrived(2, half, c)
-                back_copy(half, c).start()
-
-    add_halves(0)
+                for half in (1, 0):
+                    part_arrived(2, half, c)
+                    back_copy(half, c).start()
+
+    for c in range(0 * PER, 1 * PER):
+        add_halves(c)
     block_weights(0)
     for d in range(4):
         flip(d)
     image_part(1)
     grad_other.start()
-    add_halves(1)
+    for c in range(1 * PER, 2 * PER):
+        add_halves(c)
     image_part(0)
     grad_same.start()
-    add_halves(2)
-    relay_parts(1)
+    for c in range(2 * PER, 3 * PER):
+        add_halves(c)
 
     x = own_scores[...]
     own_col = jnp.concatenate([col_column[0]] * (R // 128), axis=1)
     own_w = jnp.exp(x - own_row_lse) + jnp.exp(x - own_col)
     weights[0, :, pl.ds(2 * R, R)] = jnp.where(mask, own_w - 2.0, own_w).astype(BF16)
     own_weights_t[...] = jnp.transpose(weights[0, :, pl.ds(2 * R, R)])
-    relay_parts(0)
+    relay_parts()
 
     text_out[...] = dot_n(weights[0], images[...])
     image_out[...] = dot_n(own_weights_t[...], texts[0])

time: 99.1 us -> 96.3 us (0.972)
  the two profiles are of different devices: /device:TPU:1 before, /device:TPU:24 now
where the time goes in v6:
time: 96.3 us; the launch traced here: 95.7 us
  Pallas kernels  90.1 us (94%)
  between operations  2.97 us (3%)
  local copies, waits for them, and re-layouts  2.55 us (3%)
    pallas_call x1, Pallas kernels, on_device(): pl.pallas_call(kernel, out_shape=(jax.ShapeDtypeStruct((1,), F32), jax.Sh...  90.1 us
    unnamed x2, local copies, waits for them, and re-layouts  2.55 us

profile of v6, /device:TPU:24, one launch (start us, length us, event | category | flops | bytes accessed | tf_op | source)
XLA Modules:
  0.0 95.7 jit_solution(2760278899672664236)
XLA Ops:
  1.3 90.1 %shard_map.67 = (f32[1]{0:T(128)}, f32[384,1280]{1,0:T(8,128)S(1)}, f32[384,1280]{1,0:T(8,128)S(1)}) custom-call(f32[1]{0:T(128)S(6)} %copy.10.scale_ref, bf16[384,1280]{1,0:T(8,128)(2,1)} %image_ref.1, bf16[384,1280]{1,0:T(8,128)(2,1)} %text_ref.1, s32[384]{0:T(512)} %pos_ref.1), custom_call_target="tpu_custom_call" | custom-call | tf_op jit(solution)/shard_map/pallas_call | solution.py:468
  92.0 1.3 %copy.12 = f32[384,1280]{1,0:T(8,128)} copy(f32[384,1280]{1,0:T(8,128)S(1)} %get-tuple-element.7) | data formatting | bytes 3932160
  93.3 1.3 %copy.13 = f32[384,1280]{1,0:T(8,128)} copy(f32[384,1280]{1,0:T(8,128)S(1)} %get-tuple-element.8) | data formatting | bytes 3932160

commit v7 on v6

--- a/solution.py
+++ b/solution.py
@@ -343,7 +343,6 @@
     stash1[...] = whole[:, :H]
     for c in range(NC):
         part_copy(part1, 0, down_slot, 1, c, down_far).start()
-    loss_send(1, loss_sum(0))
     col_lse(3)
     block_weights(3)
     whole = text_part(3)
@@ -382,6 +381,7 @@
         flip(d)
     image_part(1)
     grad_other.start()
+    loss_send(1, loss_sum(0))
     for c in range(1 * PER, 2 * PER):
         add_halves(c)
     image_part(0)

time: 96.3 us -> 95.8 us (level)
  no operation moved by 1% of the time
where the time goes in v7:
time: 95.8 us; the launch traced here: 95.7 us
  Pallas kernels  90.1 us (94%)
  between operations  2.97 us (3%)
  local copies, waits for them, and re-layouts  2.55 us (3%)
    pallas_call x1, Pallas kernels, on_device(): pl.pallas_call(kernel, out_shape=(jax.ShapeDtypeStruct((1,), F32), jax.Sh...  90.1 us
    unnamed x2, local copies, waits for them, and re-layouts  2.55 us

profile of v7, /device:TPU:24, one launch (start us, length us, event | category | flops | bytes accessed | tf_op | source)
XLA Modules:
  0.0 95.7 jit_solution(11658404804428217394)
XLA Ops:
  1.3 90.1 %shard_map.67 = (f32[1]{0:T(128)}, f32[384,1280]{1,0:T(8,128)S(1)}, f32[384,1280]{1,0:T(8,128)S(1)}) custom-call(f32[1]{0:T(128)S(6)} %copy.10.scale_ref, bf16[384,1280]{1,0:T(8,128)(2,1)} %image_ref.1, bf16[384,1280]{1,0:T(8,128)(2,1)} %text_ref.1, s32[384]{0:T(512)} %pos_ref.1), custom_call_target="tpu_custom_call" | custom-call | tf_op jit(solution)/shard_map/pallas_call | solution.py:468
  92.0 1.3 %copy.12 = f32[384,1280]{1,0:T(8,128)} copy(f32[384,1280]{1,0:T(8,128)S(1)} %get-tuple-element.7) | data formatting | bytes 3932160
  93.3 1.3 %copy.13 = f32[384,1280]{1,0:T(8,128)} copy(f32[384,1280]{1,0:T(8,128)S(1)} %get-tuple-element.8) | data formatting | bytes 3932160

commit v8 on v7

--- a/solution.py
+++ b/solution.py
@@ -374,15 +374,13 @@
                     part_arrived(2, half, c)
                     back_copy(half, c).start()
 
-    for c in range(0 * PER, 1 * PER):
-        add_halves(c)
     block_weights(0)
     for d in range(4):
         flip(d)
     image_part(1)
     grad_other.start()
     loss_send(1, loss_sum(0))
-    for c in range(1 * PER, 2 * PER):
+    for c in range(0, 2 * PER):
         add_halves(c)
     image_part(0)
     grad_same.start()

time: 95.8 us -> 95.7 us (level)
  no operation moved by 1% of the time
where the time goes in v8:
time: 95.7 us; the launch traced here: 95.5 us
  Pallas kernels  90 us (94%)
  between operations  2.97 us (3%)
  local copies, waits for them, and re-layouts  2.55 us (3%)
    pallas_call x1, Pallas kernels, on_device(): pl.pallas_call(kernel, out_shape=(jax.ShapeDtypeStruct((1,), F32), jax.Sh...  90 us
    unnamed x2, local copies, waits for them, and re-layouts  2.55 us

profile of v8, /device:TPU:24, one launch (start us, length us, event | category | flops | bytes accessed | tf_op | source)
XLA Modules:
  0.0 95.5 jit_solution(7156252905300196914)
XLA Ops:
  1.3 90.0 %shard_map.67 = (f32[1]{0:T(128)}, f32[384,1280]{1,0:T(8,128)S(1)}, f32[384,1280]{1,0:T(8,128)S(1)}) custom-call(f32[1]{0:T(128)S(6)} %copy.10.scale_ref, bf16[384,1280]{1,0:T(8,128)(2,1)} %image_ref.1, bf16[384,1280]{1,0:T(8,128)(2,1)} %text_ref.1, s32[384]{0:T(512)} %pos_ref.1), custom_call_target="tpu_custom_call" | custom-call | tf_op jit(solution)/shard_map/pallas_call | solution.py:466
  91.9 1.3 %copy.12 = f32[384,1280]{1,0:T(8,128)} copy(f32[384,1280]{1,0:T(8,128)S(1)} %get-tuple-element.7) | data formatting | bytes 3932160
  93.1 1.3 %copy.13 = f32[384,1280]{1,0:T(8,128)} copy(f32[384,1280]{1,0:T(8,128)S(1)} %get-tuple-element.8) | data formatting | bytes 3932160
